TPU v7x, 32 devices: a whole 2x2x4 slice. The times are simulated.
32 devices in a mesh: ctx: 4 (over y, x), head: 8 (over z, core).
Axes of the slice: x: 2, y: 2, z: 4, core: 2. Of those that a mesh axis runs over, the one named last changes fastest.
Arguments:
- queries: bfloat16 [1024, 128, 128], P('ctx', 'head'), may hold values from -24 to 24
- cache_keys: bfloat16 [8, 3072, 128], P(None, 'ctx'), may hold values from -12 to 12
- cache_values: bfloat16 [8, 3072, 128], P(None, 'ctx'), may hold values from -6 to 6
- scale_index: int32 [8, 24], P(None, 'ctx'), may hold values from 0 to 63
- scale_table: float32 [2, 64], replicated, may hold values from 0.6 to 1.6
- hist_lengths: int32 [4], P('ctx'), may hold values from 192 to 768, as said below
- span_offsets: int32 [8], replicated, may hold values from 0 to 3072
- new_keys: bfloat16 [1024, 8, 128], P('ctx'), may hold values from -12 to 12
- new_values: bfloat16 [1024, 8, 128], P('ctx'), may hold values from -6 to 6
- head_groups: int32 [128], P('head'), may hold values from 0 to 7, as said below
- out_weight: bfloat16 [16384, 8192], P('head'), may hold values from -0.5 to 0.5
Outputs:
- projected: bfloat16 [1024, 8192], P('ctx', 'head')
Inputs may be any that keep to these rules, and one draw needn't show every extreme that they name: `head_groups`: each key-value head serves exactly 16 query heads. `hist_lengths`: at least one block is full.
All inputs are finite; a program needn't handle non-finite values.
Results may differ from a plain program's by a relative error of at most 0.0058.
Values may be sent and summed in bfloat16 or wider, within the bound.
A program may use at most 128 MiB of HBM per device.

v0:
```python
import math

import jax
import jax.numpy as jnp
from jax import lax
from jax.sharding import PartitionSpec as P

SPAN = 128


floor_score = -1e30


def entering(part, axis, combine, identity):
    place = lax.axis_index(axis)
    gathered = lax.all_gather(part, axis)
    state = jnp.zeros_like(part) + jnp.asarray(identity, part.dtype)

    def one(hop, state):
        return combine(state, lax.dynamic_index_in_dim(gathered, hop, 0, False))

    return lax.fori_loop(0, place, one, state)


def passed_along(value, axis, steps):
    count = lax.axis_size(axis)
    pairs = [(source, (source + steps) % count) for source in range(count)]
    return lax.ppermute(value, axis, pairs)


def add_counts(earlier, later):
    return earlier + later


def shards(
    queries,
    cache_keys,
    cache_values,
    scale_index,
    scale_table,
    hist_lengths,
    span_offsets,
    new_keys,
    new_values,
    head_groups,
    out_weight,
):
    ctx_count = lax.axis_size("ctx")
    position_me = lax.axis_index("ctx")
    row_count, heads_here, head_width = queries.shape
    slot_count = cache_keys.shape[1]
    spans_here = row_count // SPAN
    inverse = 1.0 / math.sqrt(head_width)
    codes = jnp.arange(scale_table.shape[1], dtype=jnp.int32)
    one_hot = (scale_index[:, :, None] == codes[None, None, :]).astype(jnp.float32)
    block_scales = jnp.einsum("kbn,tn->tkb", one_hot, scale_table, precision=lax.Precision.HIGHEST)
    slot_scales = jnp.repeat(block_scales, slot_count // scale_index.shape[1], axis=2)
    head_scales = jnp.take(slot_scales, head_groups, axis=1)
    per_block_key_scales = head_scales[0] * inverse
    value_scales = head_scales[1]
    keys_here = jnp.take(cache_keys, head_groups, axis=0)
    values_here = jnp.take(cache_values, head_groups, axis=0)
    start_slot = entering(hist_lengths, "ctx", add_counts, jnp.zeros_like(hist_lengths))
    slot_ids = jnp.arange(slot_count, dtype=jnp.int32)
    live = slot_ids < hist_lengths[0]
    positions = start_slot[0] + slot_ids

    def block_partial(query_block, source):
        offsets = lax.dynamic_slice_in_dim(span_offsets, source * spans_here, spans_here)
        limits = jnp.repeat(offsets, SPAN)
        visible = live[None, :] & (positions[None, :] < limits[:, None])
        unscaled_scores = jnp.einsum(
            "rhd,hsd->hrs", query_block, keys_here, preferred_element_type=jnp.float32
        )
        logit_scores = unscaled_scores * per_block_key_scales[:, None, :]
        masked = jnp.where(visible[None], logit_scores, floor_score)
        block_top = jnp.max(masked, axis=2)
        block_expo = jnp.where(visible[None], jnp.exp(masked - block_top[:, :, None]), 0.0)
        any_visible = jnp.any(visible, axis=1)
        block_total = jnp.where(any_visible[None, :], jnp.sum(block_expo, axis=2), 1.0)
        weights = (block_expo * value_scales[:, None, :]).astype(jnp.bfloat16)
        mixed = jnp.einsum("hrs,hsd->rhd", weights, values_here, preferred_element_type=jnp.float32)
        mixed = mixed / jnp.transpose(block_total)[:, :, None]
        block_lse = jnp.where(any_visible[None, :], block_top + jnp.log(block_total), floor_score)
        return (mixed.astype(jnp.bfloat16), block_lse)

    def record(parts, lses, source, query_block):
        part, block_lse = block_partial(query_block, source)
        parts = lax.dynamic_update_index_in_dim(parts, part, source, 0)
        lses = lax.dynamic_update_index_in_dim(lses, block_lse, source, 0)
        return (parts, lses)

    def forward(query_block):
        return passed_along(query_block, "ctx", 1)

    parts = jnp.zeros((ctx_count, row_count, heads_here, head_width), jnp.bfloat16)
    lses = jnp.full((ctx_count, heads_here, row_count), floor_score, jnp.float32)
    parts, lses = record(parts, lses, position_me, queries)

    def one_turn(turn, carry):
        travelling, parts_now, lses_now = carry
        travelling = forward(travelling)
        parts_now, lses_now = record(
            parts_now, lses_now, (position_me - turn) % ctx_count, travelling
        )
        return (travelling, parts_now, lses_now)

    travelling, parts, lses = lax.fori_loop(1, ctx_count, one_turn, (queries, parts, lses))
    query_spans = queries.reshape(spans_here, SPAN, heads_here, head_width)
    fresh_keys = jnp.take(new_keys, head_groups, axis=1).reshape(
        spans_here, SPAN, heads_here, head_width
    )
    fresh_values = jnp.take(new_values, head_groups, axis=1).reshape(
        spans_here, SPAN, heads_here, head_width
    )
    causal = jnp.arange(SPAN)[:, None] >= jnp.arange(SPAN)[None, :]
    fresh_raw = (
        jnp.einsum("crhd,cshd->chrs", query_spans, fresh_keys, preferred_element_type=jnp.float32)
        * inverse
    )
    fresh_masked = jnp.where(causal[None, None], fresh_raw, floor_score)
    fresh_top = jnp.max(fresh_masked, axis=3)
    fresh_expo = jnp.where(causal[None, None], jnp.exp(fresh_masked - fresh_top[..., None]), 0.0)
    fresh_total = jnp.sum(fresh_expo, axis=3)
    fresh_weights = fresh_expo.astype(jnp.bfloat16)
    fresh = jnp.einsum(
        "chrs,cshd->crhd", fresh_weights, fresh_values, preferred_element_type=jnp.float32
    )
    fresh = fresh / jnp.transpose(fresh_total, (0, 2, 1))[..., None]
    fresh = fresh.reshape(row_count, heads_here, head_width)
    fresh_lse = jnp.transpose(fresh_top + jnp.log(fresh_total), (1, 0, 2)).reshape(
        heads_here, row_count
    )
    home_parts, home_lses = (
        lax.all_to_all(parts.astype(jnp.float32), "ctx", split_axis=0, concat_axis=0, tiled=True),
        lax.all_to_all(lses, "ctx", split_axis=0, concat_axis=0, tiled=True),
    )
    peak = jnp.maximum(jnp.max(home_lses, axis=0), fresh_lse)
    block_weight = jnp.exp(home_lses - peak[None])
    fresh_weight = jnp.exp(fresh_lse - peak)
    numer_all = jnp.transpose(fresh_weight)[:, :, None] * fresh
    numer_all = numer_all + jnp.sum(
        jnp.transpose(block_weight, (0, 2, 1))[..., None] * home_parts, axis=0
    )
    denom_all = fresh_weight + jnp.sum(block_weight, axis=0)
    attended = (numer_all / jnp.transpose(denom_all)[:, :, None]).astype(jnp.bfloat16)
    flat = attended.reshape(row_count, heads_here * head_width)
    mine = lax.psum_scatter(
        lax.dot_general(
            out_weight, flat, (((0,), (1,)), ((), ())), preferred_element_type=jnp.float32
        ),
        "head",
        scatter_dimension=0,
        tiled=True,
    )
    return jnp.transpose(mine).astype(jnp.bfloat16)


def solution(mesh):
    placed = (
        P("ctx", "head", None),
        P(None, "ctx", None),
        P(None, "ctx", None),
        P(None, "ctx"),
        P(),
        P("ctx"),
        P(),
        P("ctx", None, None),
        P("ctx", None, None),
        P("head"),
        P("head", None),
    )
    return jax.shard_map(
        shards, mesh=mesh, in_specs=placed, out_specs=P("ctx", "head"), check_vma=False
    )
```

profile of v0, /device:TPU:8, one launch (start us, length us, event | category | flops | bytes accessed | tf_op | source)
XLA Modules:
  0.0 410.7 jit_solution(17218948526990265932)
XLA Ops:
  11.3 7.4 %all-reduce = s32[4]{0:T(128)S(1)} all-reduce(s32[4]{0:T(128)S(1)} %dynamic-update-slice), channel_id=2, replica_groups=mesh['ctx'=4,'head'=8] {'ctx'}, use_global_device_ids=true, to_apply=%add | all-reduce | flops 4 | bytes 32
  26.8 3.5 broadcast_select_fusion
  32.7 4.1 %fusion.17 = f32[16,256]{1,0:T(8,128)S(1)} fusion(f32[16,768,256]{2,1,0:T(8,128)S(1)} %get-tuple-element.451, f32[16,256]{1,0:T(8,128)S(1)} %get-tuple-element.450, f32[16,768]{1,0:T(8,128)S(1)} %bitcast.183, pred[256,768]{0,1:T(8,128)(4,1)S(1)} %get-tuple-element.443), kind=kLoop, calls=%fused_computation.36 | loop fusion | flops 15724544 | bytes 12861440 | tf_op jit(solution)/shard_map/reduce_sum | solution.py:80
  36.9 6.9 %fusion.26 = bf16[1,256,16,128]{1,3,2,0:T(8,128)(2,1)} fusion(bf16[16,768,128]{2,1,0:T(8,128)(2,1)S(1)} %get-tuple-element.589, f32[16,768,256]{2,1,0:T(8,128)S(1)} %get-tuple-element.451, f32[16,768]{1,0:T(8,128)S(1)} %bitcast.193, f32[16,256]{1,0:T(8,128)S(1)} %get-tuple-element.450, f32[16,768]{1,0:T(8,128)S(1)} %bitcast.184, ...), kind=kOutput, calls=%fused_computation.54 | convolution fusion | flops 825229312 | bytes 17104896 | tf_op jit(solution)/shard_map/hrs,hsd->rhd/dot_general | solution.py:82
  51.5 123.4 %while.31 = (s32[]{:T(128)}, bf16[256,16,128]{2,0,1:T(8,128)(2,1)}, bf16[4,256,16,128]{3,1,2,0:T(8,128)(2,1)}, f32[4,16,256]{2,1,0:T(8,128)}, s32[]{:T(128)}, /*...) while((s32[]{:T(128)}, bf16[256,16,128]{2,0,1:T(8,128)(2,1)}, ...), condition=%wide.region_11.14_spmd.clone, body=%wide.region_7.13_spmd.clone.sunk | while | flops 1656300800 | bytes 66169564 | solution.py:108
  55.1 22.8 %collective-permute-done = bf16[256,16,128]{2,0,1:T(8,128)(2,1)} collective-permute-done((bf16[256,16,128]{2,0,1:T(8,128)(2,1)}, bf16[256,16,128]{2,0,1:T(8,128)(2,1)}, u32[]{:S(2)}, u32[]{:S(2)}) %collective-permute-start) | collective-permute-done | bytes 1048608 | tf_op jit(solution)/shard_map/while/body/eval_jaxpr/ppermute | solution.py:28
  78.0 3.2 fusion.74
  81.2 4.5 %fusion.75 = f32[16,256]{1,0:T(8,128)S(1)} fusion(f32[16,256,768]{2,1,0:T(8,128)S(1)} %get-tuple-element.556, f32[16,256]{1,0:T(8,128)S(1)} %get-tuple-element.557, f32[16,768]{1,0:T(8,128)S(1)} %get-tuple-element.623, pred[256,768]{1,0:T(8,128)(4,1)S(1)} %get-tuple-element.555), kind=kLoop, calls=%fused_computation.12.clone.1 | loop fusion | flops 15724544 | bytes 12861440 | tf_op jit(solution)/shard_map/while/body/eval_jaxpr/reduce_sum | solution.py:80
  86.3 6.2 %bitcast_dynamic-update-slice_fusion.2 = bf16[4,256,16,128]{3,1,2,0:T(8,128)(2,1)} fusion(bf16[4,256,16,128]{3,1,2,0:T(8,128)(2,1)} %get-tuple-element.600, s32[]{:T(128)S(6)} %select_n.333, f32[256,16]{0,1:T(8,128)S(1)} %select_bitcast_fusion.4, bf16[16,768,128]{2,1,0:T(8,128)(2,1)S(1)} %copy-done.7, f32[16,256,768]{2,1,0:T(8,128)S(1)} %get-tuple-element.556, ...), kind=kOutput, calls=%fused_computation.17.clone.1 | convolution fusion | flops 825229312 | bytes 17104900 | tf_op jit(solution)/shard_map/while/body/eval_jaxpr/hrs,hsd->rhd/dot_general | solution.py:82
  95.9 22.5 %collective-permute-done = bf16[256,16,128]{2,0,1:T(8,128)(2,1)} collective-permute-done((bf16[256,16,128]{2,0,1:T(8,128)(2,1)}, bf16[256,16,128]{2,0,1:T(8,128)(2,1)}, u32[]{:S(2)}, u32[]{:S(2)}) %collective-permute-start) | collective-permute-done | bytes 1048608 | tf_op jit(solution)/shard_map/while/body/eval_jaxpr/ppermute | solution.py:28
  121.7 4.5 %fusion.75 = f32[16,256]{1,0:T(8,128)S(1)} fusion(f32[16,256,768]{2,1,0:T(8,128)S(1)} %get-tuple-element.556, f32[16,256]{1,0:T(8,128)S(1)} %get-tuple-element.557, f32[16,768]{1,0:T(8,128)S(1)} %get-tuple-element.623, pred[256,768]{1,0:T(8,128)(4,1)S(1)} %get-tuple-element.555), kind=kLoop, calls=%fused_computation.12.clone.1 | loop fusion | flops 15724544 | bytes 12861440 | tf_op jit(solution)/shard_map/while/body/eval_jaxpr/reduce_sum | solution.py:80
  126.8 6.2 %bitcast_dynamic-update-slice_fusion.2 = bf16[4,256,16,128]{3,1,2,0:T(8,128)(2,1)} fusion(bf16[4,256,16,128]{3,1,2,0:T(8,128)(2,1)} %get-tuple-element.600, s32[]{:T(128)S(6)} %select_n.333, f32[256,16]{0,1:T(8,128)S(1)} %select_bitcast_fusion.4, bf16[16,768,128]{2,1,0:T(8,128)(2,1)S(1)} %copy-done.7, f32[16,256,768]{2,1,0:T(8,128)S(1)} %get-tuple-element.556, ...), kind=kOutput, calls=%fused_computation.17.clone.1 | convolution fusion | flops 825229312 | bytes 17104900 | tf_op jit(solution)/shard_map/while/body/eval_jaxpr/hrs,hsd->rhd/dot_general | solution.py:82
  136.4 21.6 %collective-permute-done = bf16[256,16,128]{2,0,1:T(8,128)(2,1)} collective-permute-done((bf16[256,16,128]{2,0,1:T(8,128)(2,1)}, bf16[256,16,128]{2,0,1:T(8,128)(2,1)}, u32[]{:S(2)}, u32[]{:S(2)}) %collective-permute-start) | collective-permute-done | bytes 1048608 | tf_op jit(solution)/shard_map/while/body/eval_jaxpr/ppermute | solution.py:28
  161.2 4.5 %fusion.75 = f32[16,256]{1,0:T(8,128)S(1)} fusion(f32[16,256,768]{2,1,0:T(8,128)S(1)} %get-tuple-element.556, f32[16,256]{1,0:T(8,128)S(1)} %get-tuple-element.557, f32[16,768]{1,0:T(8,128)S(1)} %get-tuple-element.623, pred[256,768]{1,0:T(8,128)(4,1)S(1)} %get-tuple-element.555), kind=kLoop, calls=%fused_computation.12.clone.1 | loop fusion | flops 15724544 | bytes 12861440 | tf_op jit(solution)/shard_map/while/body/eval_jaxpr/reduce_sum | solution.py:80
  166.4 6.2 %bitcast_dynamic-update-slice_fusion.2 = bf16[4,256,16,128]{3,1,2,0:T(8,128)(2,1)} fusion(bf16[4,256,16,128]{3,1,2,0:T(8,128)(2,1)} %get-tuple-element.600, s32[]{:T(128)S(6)} %select_n.333, f32[256,16]{0,1:T(8,128)S(1)} %select_bitcast_fusion.4, bf16[16,768,128]{2,1,0:T(8,128)(2,1)S(1)} %copy-done.7, f32[16,256,768]{2,1,0:T(8,128)S(1)} %get-tuple-element.556, ...), kind=kOutput, calls=%fused_computation.17.clone.1 | convolution fusion | flops 825229312 | bytes 17104900 | tf_op jit(solution)/shard_map/while/body/eval_jaxpr/hrs,hsd->rhd/dot_general | solution.py:82
  174.9 3.3 all-to-all-start
  178.2 6.5 %convert_element_type.46 = f32[4,256,16,128]{3,1,2,0:T(8,128)} convert(bf16[4,256,16,128]{3,1,2,0:T(8,128)(2,1)} %get-tuple-element.320) | non-fusion elementwise | flops 2097152 | bytes 12582912 | tf_op jit(solution)/shard_map/convert_element_type | solution.py:135
  184.7 5.8 %all-to-all-start.1 = ((f32[4,256,16,128]{3,1,2,0:T(8,128)}), f32[4,256,16,128]{3,1,2,0:T(8,128)}, u32[]{:S(2)}, u32[]{:S(2)}) async-start(f32[4,256,16,128]{3,1,2,0:T(8,128)} %convert_element_type.46), calls=%async_computation.1 | async-start | bytes 16777216 | tf_op jit(solution)/shard_map/all_to_all | solution.py:135
  190.8 3.6 gather_fusion.1
  194.4 3.6 gather_fusion.4
  204.2 74.7 %all-to-all-done.1 = f32[4,256,16,128]{3,1,2,0:T(8,128)} async-done(((f32[4,256,16,128]{3,1,2,0:T(8,128)}), f32[4,256,16,128]{3,1,2,0:T(8,128)}, u32[]{:S(2)}, u32[]{:S(2)}) %all-to-all-start.1) | async-done | bytes 8388640 | tf_op jit(solution)/shard_map/all_to_all | solution.py:135
  278.8 5.4 %multiply_reduce_fusion = f32[256,16,128]{2,0,1:T(8,128)S(1)} fusion(f32[4,256,16,128]{3,1,2,0:T(8,128)} %all-to-all-done.1, f32[4,256,16]{1,2,0:T(8,128)S(1)} %get-tuple-element.436), kind=kLoop, calls=%fused_computation.37 | loop fusion | flops 3670016 | bytes 10551296 | tf_op jit(solution)/shard_map/reduce_sum | solution.py:142
  292.8 21.8 %convolution_bitcast_fusion = f32[8192,256]{0,1:T(8,128)} fusion(bf16[2048,8192]{1,0:T(8,128)(2,1)} %param.29, f32[32,8,16,128]{3,2,1,0:T(8,128)} %bitcast.188, f32[256,2048]{1,0:T(8,128)} %copy.77, f32[32,8,16,128]{3,2,1,0:T(8,128)S(1)} %bitcast.186, f32[32,8,16,128]{3,2,1,0:T(8,128)} %bitcast.187), kind=kOutput, calls=%fused_computation.35 | convolution fusion | flops 8592031744 | bytes 50331648 | tf_op jit(solution)/shard_map/dot_general | solution.py:149
  314.7 87.1 %reduce-scatter.2.cloned.1.call-done = f32[1024,256]{0,1:T(8,128)} async-done(((f32[8192,256]{0,1:T(8,128)}), f32[1024,256]{0,1:T(8,128)}) %reduce-scatter.2.cloned.1.call-update) | async-done | bytes 1048592 | tf_op jit(solution)/shard_map/reduce_scatter | solution.py:148
  (115 shorter events, 60.4 us)
Async XLA Ops:
  6.5 12.2 %copy-start = (bf16[8,768,128]{2,1,0:T(8,128)(2,1)S(1)}, bf16[8,768,128]{2,1,0:T(8,128)(2,1)}, u32[]{:S(2)}) copy-start(bf16[8,768,128]{2,1,0:T(8,128)(2,1)} %param.21) | copy-start | bytes 4718596
  18.7 2.7 copy-start.4
  21.4 2.6 copy-start.12
  21.4 2.7 copy-start.13
  21.4 4.1 copy-start.9
  26.8 3.9 copy-start.10
  30.4 6.5 %copy-start.6 = (bf16[16,768,128]{2,1,0:T(8,128)(2,1)}, bf16[16,768,128]{2,1,0:T(8,128)(2,1)S(1)}, u32[]{:S(2)}) copy-start(bf16[16,768,128]{2,1,0:T(8,128)(2,1)S(1)} %get-tuple-element.589) | copy-start | bytes 9437188
  46.1 4.2 %copy-start.5 = (bf16[1,256,16,128]{3,1,2,0:T(8,128)(2,1)S(1)}, bf16[1,256,16,128]{3,1,2,0:T(8,128)(2,1)}, u32[]{:S(2)}) copy-start(bf16[1,256,16,128]{3,1,2,0:T(8,128)(2,1)} %copy.69) | copy-start | bytes 3145732
  47.3 4.1 %copy-start.14 = (s32[8]{0:T(128)S(1)}, s32[8]{0:T(128)}, u32[]{:S(2)}) copy-start(s32[8]{0:T(128)} %param.25) | copy-start | bytes 100
  51.5 26.5 %collective-permute-start = (bf16[256,16,128]{2,0,1:T(8,128)(2,1)}, bf16[256,16,128]{2,0,1:T(8,128)(2,1)}, u32[]{:S(2)}, u32[]{:S(2)}) collective-permute-start(bf16[256,16,128]{2,0,1:T(8,128)(2,1)} %get-tuple-element.599), channel_id=1, source_target_pairs={{0,8},{8,16},{16,24},{24,0},{1,9},{9,17},{17,25},{25,1},{2,10},{10... | collective-permute-start | bytes 3145736 | tf_op jit(solution)/shard_map/while/body/eval_jaxpr/ppermute | solution.py:28
  81.2 5.1 %copy-start.7 = (bf16[16,768,128]{2,1,0:T(8,128)(2,1)S(1)}, bf16[16,768,128]{2,1,0:T(8,128)(2,1)}, u32[]{:S(2)}) copy-start(bf16[16,768,128]{2,1,0:T(8,128)(2,1)} %get-tuple-element.625) | copy-start | bytes 9437188 | tf_op jit(solution)/shard_map/while
  94.8 23.7 %collective-permute-start = (bf16[256,16,128]{2,0,1:T(8,128)(2,1)}, bf16[256,16,128]{2,0,1:T(8,128)(2,1)}, u32[]{:S(2)}, u32[]{:S(2)}) collective-permute-start(bf16[256,16,128]{2,0,1:T(8,128)(2,1)} %get-tuple-element.599), channel_id=1, source_target_pairs={{0,8},{8,16},{16,24},{24,0},{1,9},{9,17},{17,25},{25,1},{2,10},{10... | collective-permute-start | bytes 3145736 | tf_op jit(solution)/shard_map/while/body/eval_jaxpr/ppermute | solution.py:28
  121.7 5.1 %copy-start.7 = (bf16[16,768,128]{2,1,0:T(8,128)(2,1)S(1)}, bf16[16,768,128]{2,1,0:T(8,128)(2,1)}, u32[]{:S(2)}) copy-start(bf16[16,768,128]{2,1,0:T(8,128)(2,1)} %get-tuple-element.625) | copy-start | bytes 9437188 | tf_op jit(solution)/shard_map/while
  135.3 22.7 %collective-permute-start = (bf16[256,16,128]{2,0,1:T(8,128)(2,1)}, bf16[256,16,128]{2,0,1:T(8,128)(2,1)}, u32[]{:S(2)}, u32[]{:S(2)}) collective-permute-start(bf16[256,16,128]{2,0,1:T(8,128)(2,1)} %get-tuple-element.599), channel_id=1, source_target_pairs={{0,8},{8,16},{16,24},{24,0},{1,9},{9,17},{17,25},{25,1},{2,10},{10... | collective-permute-start | bytes 3145736 | tf_op jit(solution)/shard_map/while/body/eval_jaxpr/ppermute | solution.py:28
  161.2 5.1 %copy-start.7 = (bf16[16,768,128]{2,1,0:T(8,128)(2,1)S(1)}, bf16[16,768,128]{2,1,0:T(8,128)(2,1)}, u32[]{:S(2)}) copy-start(bf16[16,768,128]{2,1,0:T(8,128)(2,1)} %get-tuple-element.625) | copy-start | bytes 9437188 | tf_op jit(solution)/shard_map/while
  174.9 9.8 %all-to-all-start = ((f32[4,16,256]{2,1,0:T(8,128)}), f32[4,16,256]{2,1,0:T(8,128)S(1)}, u32[]{:S(2)}, u32[]{:S(2)}) async-start(f32[4,16,256]{2,1,0:T(8,128)} %get-tuple-element.319), calls=%async_computation | async-start | bytes 131072 | tf_op jit(solution)/shard_map/all_to_all | solution.py:136
  184.7 6.1 %copy-start.2 = (bf16[256,8,128]{2,1,0:T(8,128)(2,1)S(1)}, bf16[256,8,128]{2,1,0:T(8,128)(2,1)}, u32[]{:S(2)}) copy-start(bf16[256,8,128]{2,1,0:T(8,128)(2,1)} %param.26) | copy-start | bytes 1572868
  184.7 94.2 %all-to-all-start.1 = ((f32[4,256,16,128]{3,1,2,0:T(8,128)}), f32[4,256,16,128]{3,1,2,0:T(8,128)}, u32[]{:S(2)}, u32[]{:S(2)}) async-start(f32[4,256,16,128]{3,1,2,0:T(8,128)} %convert_element_type.46), calls=%async_computation.1 | async-start | bytes 16777216 | tf_op jit(solution)/shard_map/all_to_all | solution.py:135
  190.5 3.9 copy-start.3
  190.5 211.3 %reduce-scatter.2.cloned.1.call-start = ((), (), s32[]{:S(2)}) async-start(), calls=%async_computation.3 | async-start | bytes 9437184 | tf_op jit(solution)/shard_map/reduce_scatter | solution.py:148
  198.0 1.2 copy-start.11
  289.0 3.9 copy-start.8
  314.7 89.2 %copy-start.1 = (bf16[8,768,128]{2,1,0:T(8,128)(2,1)S(1)}, bf16[8,768,128]{2,1,0:T(8,128)(2,1)}, u32[]{:S(2)}) copy-start(bf16[8,768,128]{2,1,0:T(8,128)(2,1)} %param.21) | copy-start | bytes 4718596
Sparse Core Ops, SparseCore 0:
  314.8 86.9 reduce-scatter.1
where the time goes:
time: 416 us; the launch traced here: 411 us
  waiting for transfers between devices  229 us (55%)
  matrix products  61 us (15%)
  local copies, waits for them, and re-layouts  44 us (11%)
  other arithmetic  43.2 us (10%)
  between operations  14.3 us (3%)
  starting transfers between devices  12 us (3%)
  blocking collectives  7.37 us (2%)
    reduce_scatter x1, waiting for transfers between devices, shards(): lax.psum_scatter(lax.dot_general(out_weight, flat, (((0,), (1,)), ((), ()...  87.1 us
    all_to_all x1, waiting for transfers between devices, shards(): lax.all_to_all(parts.astype(jnp.float32), 'ctx', split_axis=0, concat_axi...  74.7 us
    ppermute x3, waiting for transfers between devices, passed_along(): return lax.ppermute(value, axis, pairs)  67 us
    dot_general x4, matrix products, block_partial(): jnp.einsum('hrs,hsd->rhd', weights, values_here, preferred_element_type=j...  25.4 us
    dot_general x1, matrix products, shards(): lax.dot_general(out_weight, flat, (((0,), (1,)), ((), ())), preferred_ele...  21.8 us
    reduce_sum x4, other arithmetic, block_partial(): jnp.sum(block_expo, axis=2)  17.5 us
    dot_general x4, matrix products, block_partial(): jnp.einsum('rhd,hsd->hrs', query_block, keys_here, preferred_element_type...  11.7 us
  transfers between devices with their start and end apart: 6, of which 5 were waited for; matrix products, arithmetic and copies ran while one was open for 5% of the time, Pallas kernels for 0%

commit v1 on v0

--- a/solution.py
+++ b/solution.py
@@ -3,7 +3,11 @@
 import jax
 import jax.numpy as jnp
 from jax import lax
+from jax.experimental import pallas as pl
+from jax.experimental.pallas import tpu as pltpu
 from jax.sharding import PartitionSpec as P
+
+MESH = pl.DeviceIdType.MESH
 
 SPAN = 128
 
@@ -30,6 +34,226 @@
 
 def add_counts(earlier, later):
     return earlier + later
+
+
+def project_and_reduce(flat, out_weight):
+    heads = lax.axis_size("head")
+    planes = heads // 2
+    rows, depth = flat.shape
+    width = out_weight.shape[1] // heads
+    pieces = 4
+    piece = rows // pieces
+    tile = 256
+    slots = 4
+    order = [
+        sorted(range(planes), key=lambda d, z=z: (-abs(d - z), -d if z < planes // 2 else d))
+        for z in range(planes)
+    ]
+
+    def kernel(
+        flat_ref, weight_ref, out_ref, weights, own, pair_out, pair_in,
+        up_out, up_in, down_out, down_in,
+        weight_sem, pair_send, pair_recv, up_send, up_recv, down_send, down_recv,
+    ):
+        me = lax.axis_index("head")
+        plane = me // 2
+        core = me % 2
+        sibling = {"head": 2 * plane + 1 - core}
+        above = {"head": me + 2}
+        below = {"head": me - 2}
+        has_above = plane < planes - 1
+        has_below = plane > 0
+
+        def target(step):
+            d = jnp.int32(order[0][step])
+            for z in range(1, planes):
+                d = jnp.where(plane == z, order[z][step], d)
+            return d
+
+        targets = [target(step) for step in range(planes)]
+        blocks = []
+        for d in targets:
+            blocks += [2 * d + 1 - core, 2 * d + core]
+
+        def fetch(i):
+            column = pl.multiple_of(blocks[i] * width, width)
+            return pltpu.make_async_copy(
+                weight_ref.at[:, pl.ds(column, width)], weights.at[i % slots], weight_sem.at[i % slots]
+            )
+
+        for i in range(slots - 1):
+            fetch(i).start()
+
+        barrier = pltpu.get_barrier_semaphore()
+        pl.semaphore_signal(barrier, inc=1, device_id=sibling, device_id_type=MESH)
+
+        @pl.when(has_above)
+        def _():
+            pl.semaphore_signal(barrier, inc=1, device_id=above, device_id_type=MESH)
+
+        @pl.when(has_below)
+        def _():
+            pl.semaphore_signal(barrier, inc=1, device_id=below, device_id_type=MESH)
+
+        pl.semaphore_wait(barrier, 1 + has_above.astype(jnp.int32) + has_below.astype(jnp.int32))
+
+        def to_sibling(d):
+            return pltpu.make_async_remote_copy(
+                src_ref=pair_out.at[d], dst_ref=pair_in.at[d],
+                send_sem=pair_send.at[d], recv_sem=pair_recv.at[d],
+                device_id=sibling, device_id_type=MESH,
+            )
+
+        def upward(d, p):
+            return pltpu.make_async_remote_copy(
+                src_ref=up_out.at[d, p], dst_ref=up_in.at[d, p],
+                send_sem=up_send.at[d, p], recv_sem=up_recv.at[d, p],
+                device_id=above, device_id_type=MESH,
+            )
+
+        def downward(d, p):
+            return pltpu.make_async_remote_copy(
+                src_ref=down_out.at[d, p], dst_ref=down_in.at[d, p],
+                send_sem=down_send.at[d, p], recv_sem=down_recv.at[d, p],
+                device_id=below, device_id_type=MESH,
+            )
+
+        def multiply(i, store):
+            if i + slots - 1 < len(blocks):
+                fetch(i + slots - 1).start()
+            fetch(i).wait()
+
+            @pl.loop(0, width // tile)
+            def _(t):
+                columns = pl.ds(pl.multiple_of(t * tile, tile), tile)
+                store(
+                    columns,
+                    jnp.dot(
+                        flat_ref[...], weights[i % slots, :, columns],
+                        preferred_element_type=jnp.float32,
+                    ),
+                )
+
+        def combine(d):
+            to_sibling(d).wait_recv()
+
+            @pl.loop(0, pieces)
+            def _(p):
+                span = pl.ds(pl.multiple_of(p * piece, piece), piece)
+
+                @pl.when(d > plane)
+                def _():
+                    total = own[d, span] + pair_in[d, span].astype(jnp.float32)
+
+                    @pl.when(has_below)
+                    def _():
+                        upward(d, p).wait_recv()
+                        up_out[d, p] = (total + up_in[d, p].astype(jnp.float32)).astype(jnp.bfloat16)
+
+                    @pl.when(jnp.logical_not(has_below))
+                    def _():
+                        up_out[d, p] = total.astype(jnp.bfloat16)
+
+                    upward(d, p).start()
+
+                @pl.when(d < plane)
+                def _():
+                    total = own[d, span] + pair_in[d, span].astype(jnp.float32)
+
+                    @pl.when(has_above)
+                    def _():
+                        downward(d, p).wait_recv()
+                        down_out[d, p] = (total + down_in[d, p].astype(jnp.float32)).astype(
+                            jnp.bfloat16
+                        )
+
+                    @pl.when(jnp.logical_not(has_above))
+                    def _():
+                        down_out[d, p] = total.astype(jnp.bfloat16)
+
+                    downward(d, p).start()
+
+                @pl.when(d == plane)
+                def _():
+                    own[d, span] = own[d, span] + pair_in[d, span].astype(jnp.float32)
+
+                    @pl.when(has_below)
+                    def _():
+                        upward(d, p).wait_recv()
+                        own[d, span] = own[d, span] + up_in[d, p].astype(jnp.float32)
+
+                    @pl.when(has_above)
+                    def _():
+                        downward(d, p).wait_recv()
+                        own[d, span] = own[d, span] + down_in[d, p].astype(jnp.float32)
+
+                    out_ref[span] = own[d, span].astype(jnp.bfloat16)
+
+        for step in range(planes):
+            d = targets[step]
+
+            def to_pair(columns, value, d=d):
+                pair_out[d, :, columns] = value.astype(jnp.bfloat16)
+
+            def to_own(columns, value, d=d):
+                own[d, :, columns] = value
+
+            multiply(2 * step, to_pair)
+            to_sibling(d).start()
+            multiply(2 * step + 1, to_own)
+            if step > 0:
+                combine(targets[step - 1])
+        combine(targets[planes - 1])
+
+        for step in range(planes):
+            d = targets[step]
+            to_sibling(d).wait_send()
+
+            @pl.loop(0, pieces)
+            def _(p, d=d):
+                @pl.when(d > plane)
+                def _():
+                    upward(d, p).wait_send()
+
+                @pl.when(d < plane)
+                def _():
+                    downward(d, p).wait_send()
+
+    block = (planes, rows, width)
+    cut = (planes, pieces, piece, width)
+    dma = pltpu.SemaphoreType.DMA
+    return pl.pallas_call(
+        kernel,
+        out_shape=jax.ShapeDtypeStruct((rows, width), jnp.bfloat16),
+        in_specs=[pl.BlockSpec(memory_space=pltpu.VMEM), pl.BlockSpec(memory_space=pl.ANY)],
+        out_specs=pl.BlockSpec(memory_space=pltpu.VMEM),
+        scratch_shapes=[
+            pltpu.VMEM((slots, depth, width), jnp.bfloat16),
+            pltpu.VMEM(block, jnp.float32),
+            pltpu.VMEM(block, jnp.bfloat16),
+            pltpu.VMEM(block, jnp.bfloat16),
+            pltpu.VMEM(cut, jnp.bfloat16),
+            pltpu.VMEM(cut, jnp.bfloat16),
+            pltpu.VMEM(cut, jnp.bfloat16),
+            pltpu.VMEM(cut, jnp.bfloat16),
+            dma((slots,)),
+            dma((planes,)),
+            dma((planes,)),
+            dma((planes, pieces)),
+            dma((planes, pieces)),
+            dma((planes, pieces)),
+            dma((planes, pieces)),
+        ],
+        compiler_params=pltpu.CompilerParams(
+            collective_id=1, has_side_effects=True, vmem_limit_bytes=56 * 1024 * 1024
+        ),
+        cost_estimate=pl.CostEstimate(
+            flops=2 * rows * depth * width * heads,
+            bytes_accessed=2 * depth * width * heads,
+            transcendentals=0,
+        ),
+        name="project_and_reduce",
+    )(flat, out_weight)
 
 
 def shards(
@@ -145,15 +369,7 @@
     denom_all = fresh_weight + jnp.sum(block_weight, axis=0)
     attended = (numer_all / jnp.transpose(denom_all)[:, :, None]).astype(jnp.bfloat16)
     flat = attended.reshape(row_count, heads_here * head_width)
-    mine = lax.psum_scatter(
-        lax.dot_general(
-            out_weight, flat, (((0,), (1,)), ((), ())), preferred_element_type=jnp.float32
-        ),
-        "head",
-        scatter_dimension=0,
-        tiled=True,
-    )
-    return jnp.transpose(mine).astype(jnp.bfloat16)
+    return project_and_reduce(flat, out_weight)
 
 
 def solution(mesh):

time: 416 us -> 338 us (0.81)
  waiting for transfers between devices: 229 us -> 140 us
  Pallas kernels: 0 us -> 49.4 us
  matrix products: 61 us -> 40.5 us
  between operations: 14.3 us -> 0.95 us
  local copies, waits for them, and re-layouts: 44 us -> 38.3 us
    reduce_scatter x1 -> x0, waiting for transfers between devices: 87.1 us -> none  [shards(): lax.psum_scatter(lax.dot_general(out_weight, flat, (((0,), (1,)), ((), ()...]
    pallas_call x0 -> x1, Pallas kernels: none -> 49.4 us  [project_and_reduce(): pl.pallas_call(kernel, out_shape=jax.ShapeDtypeStruct((rows, width), jnp....]
    dot_general x1 -> x0, matrix products: 21.8 us -> none  [shards(): lax.dot_general(out_weight, flat, (((0,), (1,)), ((), ())), preferred_ele...]
    reduce_sum x2 -> x0, local copies, waits for them, and re-layouts: 4.77 us -> none  [shards(): jnp.sum(jnp.transpose(block_weight, (0, 2, 1))[..., None] * home_parts, a...]
  transfers between devices with their start and end apart: 6 -> 5, of which waited for: 5 -> 4; matrix products, arithmetic and copies ran while one was open for 5% -> 7% of each run, Pallas kernels for 0% -> 0%
where the time goes in v1:
time: 338 us; the launch traced here: 333 us
  waiting for transfers between devices  140 us (41%)
  Pallas kernels  49.4 us (15%)
  other arithmetic  44.3 us (13%)
  matrix products  40.5 us (12%)
  local copies, waits for them, and re-layouts  38.3 us (11%)
  starting transfers between devices  11.9 us (4%)
  blocking collectives  7.37 us (2%)
    all_to_all x1, waiting for transfers between devices, shards(): lax.all_to_all(parts.astype(jnp.float32), 'ctx', split_axis=0, concat_axi...  73.5 us
    ppermute x3, waiting for transfers between devices, passed_along(): return lax.ppermute(value, axis, pairs)  67 us
    pallas_call x1, Pallas kernels, project_and_reduce(): pl.pallas_call(kernel, out_shape=jax.ShapeDtypeStruct((rows, width), jnp....  49.4 us
    dot_general x4, matrix products, block_partial(): jnp.einsum('hrs,hsd->rhd', weights, values_here, preferred_element_type=j...  25.4 us
    reduce_sum x4, other arithmetic, block_partial(): jnp.sum(block_expo, axis=2)  17.5 us
    dot_general x4, matrix products, block_partial(): jnp.einsum('rhd,hsd->hrs', query_block, keys_here, preferred_element_type...  11.7 us
    unnamed x1, blocking collectives  7.37 us
    while x9, local copies, waits for them, and re-layouts  7 us
  transfers between devices with their start and end apart: 5, of which 4 were waited for; matrix products, arithmetic and copies ran while one was open for 7% of the time, Pallas kernels for 0%

profile of v1, /device:TPU:8, one launch (start us, length us, event | category | flops | bytes accessed | tf_op | source)
XLA Modules:
  0.0 333.5 jit_solution(15932281228458405841)
XLA Ops:
  4.8 7.4 %all-reduce = s32[4]{0:T(128)S(1)} all-reduce(s32[4]{0:T(128)S(1)} %dynamic-update-slice), channel_id=2, replica_groups=mesh['ctx'=4,'head'=8] {'ctx'}, use_global_device_ids=true, to_apply=%add | all-reduce | flops 4 | bytes 32
  20.3 3.5 %broadcast_select_fusion = (bf16[16,768,128]{2,1,0:T(8,128)(2,1)S(1)}, bf16[16,768,128]{2,1,0:T(8,128)(2,1)S(1)}) fusion(bf16[16,768,128]{2,1,0:T(8,128)(2,1)} %gather_fusion.3, pred[16]{0:T(512)(128)(4,1)S(1)} %compare_and_fusion.2, bf16[16,768,128]{2,1,0:T(8,128)(2,1)} %gather_fusion.2), kind=kLoop, calls=%fused_computation.39 | loop fusion | flops 3145728 | bytes 12582928 | tf_op jit(solution)/shard_map/jit(_take)/select_n | solution.py:285
  26.2 4.1 %fusion.17 = f32[16,256]{1,0:T(8,128)S(1)} fusion(f32[16,768,256]{2,1,0:T(8,128)S(1)} %get-tuple-element.439, f32[16,256]{1,0:T(8,128)S(1)} %get-tuple-element.438, f32[16,768]{1,0:T(8,128)S(1)} %bitcast.181, pred[256,768]{0,1:T(8,128)(4,1)S(1)} %get-tuple-element.431), kind=kLoop, calls=%fused_computation.35 | loop fusion | flops 15724544 | bytes 12861440 | tf_op jit(solution)/shard_map/reduce_sum | solution.py:304
  30.3 6.9 %fusion.26 = bf16[1,256,16,128]{1,3,2,0:T(8,128)(2,1)} fusion(bf16[16,768,128]{2,1,0:T(8,128)(2,1)S(1)} %get-tuple-element.577, f32[16,768,256]{2,1,0:T(8,128)S(1)} %get-tuple-element.439, f32[16,768]{1,0:T(8,128)S(1)} %bitcast.188, f32[16,256]{1,0:T(8,128)S(1)} %get-tuple-element.438, f32[16,768]{1,0:T(8,128)S(1)} %bitcast.182, ...), kind=kOutput, calls=%fused_computation.53 | convolution fusion | flops 825229312 | bytes 17104896 | tf_op jit(solution)/shard_map/hrs,hsd->rhd/dot_general | solution.py:306
  44.9 123.4 %while.31 = (s32[]{:T(128)}, bf16[256,16,128]{2,0,1:T(8,128)(2,1)}, bf16[4,256,16,128]{3,1,2,0:T(8,128)(2,1)}, f32[4,16,256]{2,1,0:T(8,128)}, s32[]{:T(128)}, /*...) while((s32[]{:T(128)}, bf16[256,16,128]{2,0,1:T(8,128)(2,1)}, ...), condition=%wide.region_11.14_spmd.clone, body=%wide.region_7.13_spmd.clone.sunk | while | flops 1656300800 | bytes 66169564 | solution.py:332
  48.6 22.8 %collective-permute-done = bf16[256,16,128]{2,0,1:T(8,128)(2,1)} collective-permute-done((bf16[256,16,128]{2,0,1:T(8,128)(2,1)}, bf16[256,16,128]{2,0,1:T(8,128)(2,1)}, u32[]{:S(2)}, u32[]{:S(2)}) %collective-permute-start) | collective-permute-done | bytes 1048608 | tf_op jit(solution)/shard_map/while/body/eval_jaxpr/ppermute | solution.py:32
  71.4 3.2 fusion.73
  74.7 4.5 %fusion.74 = f32[16,256]{1,0:T(8,128)S(1)} fusion(f32[16,256,768]{2,1,0:T(8,128)S(1)} %get-tuple-element.544, f32[16,256]{1,0:T(8,128)S(1)} %get-tuple-element.545, f32[16,768]{1,0:T(8,128)S(1)} %get-tuple-element.611, pred[256,768]{1,0:T(8,128)(4,1)S(1)} %get-tuple-element.543), kind=kLoop, calls=%fused_computation.12.clone.1 | loop fusion | flops 15724544 | bytes 12861440 | tf_op jit(solution)/shard_map/while/body/eval_jaxpr/reduce_sum | solution.py:304
  79.8 6.2 %bitcast_dynamic-update-slice_fusion.2 = bf16[4,256,16,128]{3,1,2,0:T(8,128)(2,1)} fusion(bf16[4,256,16,128]{3,1,2,0:T(8,128)(2,1)} %get-tuple-element.588, s32[]{:T(128)S(6)} %select_n.333, f32[256,16]{0,1:T(8,128)S(1)} %select_bitcast_fusion.4, bf16[16,768,128]{2,1,0:T(8,128)(2,1)S(1)} %copy-done.7, f32[16,256,768]{2,1,0:T(8,128)S(1)} %get-tuple-element.544, ...), kind=kOutput, calls=%fused_computation.17.clone.1 | convolution fusion | flops 825229312 | bytes 17104900 | tf_op jit(solution)/shard_map/while/body/eval_jaxpr/hrs,hsd->rhd/dot_general | solution.py:306
  89.4 22.5 %collective-permute-done = bf16[256,16,128]{2,0,1:T(8,128)(2,1)} collective-permute-done((bf16[256,16,128]{2,0,1:T(8,128)(2,1)}, bf16[256,16,128]{2,0,1:T(8,128)(2,1)}, u32[]{:S(2)}, u32[]{:S(2)}) %collective-permute-start) | collective-permute-done | bytes 1048608 | tf_op jit(solution)/shard_map/while/body/eval_jaxpr/ppermute | solution.py:32
  111.9 3.2 fusion.73
  115.1 4.5 %fusion.74 = f32[16,256]{1,0:T(8,128)S(1)} fusion(f32[16,256,768]{2,1,0:T(8,128)S(1)} %get-tuple-element.544, f32[16,256]{1,0:T(8,128)S(1)} %get-tuple-element.545, f32[16,768]{1,0:T(8,128)S(1)} %get-tuple-element.611, pred[256,768]{1,0:T(8,128)(4,1)S(1)} %get-tuple-element.543), kind=kLoop, calls=%fused_computation.12.clone.1 | loop fusion | flops 15724544 | bytes 12861440 | tf_op jit(solution)/shard_map/while/body/eval_jaxpr/reduce_sum | solution.py:304
  120.3 6.2 %bitcast_dynamic-update-slice_fusion.2 = bf16[4,256,16,128]{3,1,2,0:T(8,128)(2,1)} fusion(bf16[4,256,16,128]{3,1,2,0:T(8,128)(2,1)} %get-tuple-element.588, s32[]{:T(128)S(6)} %select_n.333, f32[256,16]{0,1:T(8,128)S(1)} %select_bitcast_fusion.4, bf16[16,768,128]{2,1,0:T(8,128)(2,1)S(1)} %copy-done.7, f32[16,256,768]{2,1,0:T(8,128)S(1)} %get-tuple-element.544, ...), kind=kOutput, calls=%fused_computation.17.clone.1 | convolution fusion | flops 825229312 | bytes 17104900 | tf_op jit(solution)/shard_map/while/body/eval_jaxpr/hrs,hsd->rhd/dot_general | solution.py:306
  129.9 21.6 %collective-permute-done = bf16[256,16,128]{2,0,1:T(8,128)(2,1)} collective-permute-done((bf16[256,16,128]{2,0,1:T(8,128)(2,1)}, bf16[256,16,128]{2,0,1:T(8,128)(2,1)}, u32[]{:S(2)}, u32[]{:S(2)}) %collective-permute-start) | collective-permute-done | bytes 1048608 | tf_op jit(solution)/shard_map/while/body/eval_jaxpr/ppermute | solution.py:32
  154.7 4.5 %fusion.74 = f32[16,256]{1,0:T(8,128)S(1)} fusion(f32[16,256,768]{2,1,0:T(8,128)S(1)} %get-tuple-element.544, f32[16,256]{1,0:T(8,128)S(1)} %get-tuple-element.545, f32[16,768]{1,0:T(8,128)S(1)} %get-tuple-element.611, pred[256,768]{1,0:T(8,128)(4,1)S(1)} %get-tuple-element.543), kind=kLoop, calls=%fused_computation.12.clone.1 | loop fusion | flops 15724544 | bytes 12861440 | tf_op jit(solution)/shard_map/while/body/eval_jaxpr/reduce_sum | solution.py:304
  159.8 6.2 %bitcast_dynamic-update-slice_fusion.2 = bf16[4,256,16,128]{3,1,2,0:T(8,128)(2,1)} fusion(bf16[4,256,16,128]{3,1,2,0:T(8,128)(2,1)} %get-tuple-element.588, s32[]{:T(128)S(6)} %select_n.333, f32[256,16]{0,1:T(8,128)S(1)} %select_bitcast_fusion.4, bf16[16,768,128]{2,1,0:T(8,128)(2,1)S(1)} %copy-done.7, f32[16,256,768]{2,1,0:T(8,128)S(1)} %get-tuple-element.544, ...), kind=kOutput, calls=%fused_computation.17.clone.1 | convolution fusion | flops 825229312 | bytes 17104900 | tf_op jit(solution)/shard_map/while/body/eval_jaxpr/hrs,hsd->rhd/dot_general | solution.py:306
  168.3 3.3 all-to-all-start
  171.6 6.5 %convert_element_type.40 = f32[4,256,16,128]{3,1,2,0:T(8,128)} convert(bf16[4,256,16,128]{3,1,2,0:T(8,128)(2,1)} %get-tuple-element.320) | non-fusion elementwise | flops 2097152 | bytes 12582912 | tf_op jit(solution)/shard_map/convert_element_type | solution.py:359
  178.1 6.0 %all-to-all-start.1 = ((f32[4,256,16,128]{3,1,2,0:T(8,128)}), f32[4,256,16,128]{3,1,2,0:T(8,128)}, u32[]{:S(2)}, u32[]{:S(2)}) async-start(f32[4,256,16,128]{3,1,2,0:T(8,128)} %convert_element_type.40), calls=%async_computation.1 | async-start | bytes 16777216 | tf_op jit(solution)/shard_map/all_to_all | solution.py:359
  184.2 3.6 %gather_fusion.1 = bf16[16,256,128]{2,0,1:T(8,128)(2,1)S(1)} fusion(bf16[256,8,128]{2,1,0:T(8,128)(2,1)S(1)} %copy-done.2, s32[1024]{0:T(1024)S(1)} %pad_clamp_fusion), kind=kCustom, calls=%fused_computation.clone | custom fusion | bytes 2097216 | tf_op jit(solution)/shard_map/jit(_take)/gather | solution.py:334
  187.8 3.6 %gather_fusion.4 = bf16[16,256,128]{2,0,1:T(8,128)(2,1)S(1)} fusion(bf16[256,8,128]{2,1,0:T(8,128)(2,1)S(1)} %copy-done.3, s32[1024]{0:T(1024)S(1)} %pad_clamp_fusion), kind=kCustom, calls=%fused_computation.2.clone | custom fusion | bytes 2097216 | tf_op jit(solution)/shard_map/jit(_take)/gather | solution.py:337
  198.9 73.5 %all-to-all-done.1 = f32[4,256,16,128]{3,1,2,0:T(8,128)} async-done(((f32[4,256,16,128]{3,1,2,0:T(8,128)}), f32[4,256,16,128]{3,1,2,0:T(8,128)}, u32[]{:S(2)}, u32[]{:S(2)}) %all-to-all-start.1) | async-done | bytes 8388640 | tf_op jit(solution)/shard_map/all_to_all | solution.py:359
  272.4 5.6 %multiply_reduce_fusion = f32[256,16,128]{2,0,1:T(8,128)S(1)} fusion(f32[4,256,16,128]{3,1,2,0:T(8,128)} %all-to-all-done.1, f32[4,256,16]{1,2,0:T(8,128)S(1)} %get-tuple-element.424), kind=kLoop, calls=%fused_computation.36 | loop fusion | flops 3670016 | bytes 10551296 | tf_op jit(solution)/shard_map/reduce_sum | solution.py:366
  282.2 49.4 %project_and_reduce.1 = bf16[256,1024]{1,0:T(8,128)(2,1)} custom-call(bf16[256,2048]{1,0:T(8,128)(2,1)} %fusion.20.flat_ref, bf16[2048,8192]{1,0:T(8,128)(2,1)} %weight_ref.1), custom_call_target="tpu_custom_call" | custom-call | flops 8589934592 | bytes 33554432 | tf_op jit(solution)/shard_map/project_and_reduce/pallas_call | solution.py:225
  (109 shorter events, 53.5 us)
Async XLA Ops:
  0.0 12.2 %copy-start = (bf16[8,768,128]{2,1,0:T(8,128)(2,1)S(1)}, bf16[8,768,128]{2,1,0:T(8,128)(2,1)}, u32[]{:S(2)}) copy-start(bf16[8,768,128]{2,1,0:T(8,128)(2,1)} %param.21) | copy-start | bytes 4718596
  12.2 2.7 copy-start.4
  14.9 2.6 copy-start.11
  14.9 2.7 copy-start.12
  14.9 4.1 %copy-start.8 = (bf16[256,16,128]{2,1,0:T(8,128)(2,1)S(1)}, bf16[256,16,128]{2,1,0:T(8,128)(2,1)}, u32[]{:S(2)}) copy-start(bf16[256,16,128]{2,1,0:T(8,128)(2,1)} %param.19) | copy-start | bytes 3145732
  20.3 3.9 %copy-start.9 = (bf16[256,16,128]{2,1,0:T(8,128)(2,1)S(1)}, bf16[256,16,128]{2,1,0:T(8,128)(2,1)}, u32[]{:S(2)}) copy-start(bf16[256,16,128]{2,1,0:T(8,128)(2,1)} %param.19) | copy-start | bytes 3145732
  23.8 6.5 %copy-start.6 = (bf16[16,768,128]{2,1,0:T(8,128)(2,1)}, bf16[16,768,128]{2,1,0:T(8,128)(2,1)S(1)}, u32[]{:S(2)}) copy-start(bf16[16,768,128]{2,1,0:T(8,128)(2,1)S(1)} %get-tuple-element.577) | copy-start | bytes 9437188
  39.5 4.2 %copy-start.5 = (bf16[1,256,16,128]{3,1,2,0:T(8,128)(2,1)S(1)}, bf16[1,256,16,128]{3,1,2,0:T(8,128)(2,1)}, u32[]{:S(2)}) copy-start(bf16[1,256,16,128]{3,1,2,0:T(8,128)(2,1)} %copy.53) | copy-start | bytes 3145732
  40.8 4.1 %copy-start.13 = (s32[8]{0:T(128)S(1)}, s32[8]{0:T(128)}, u32[]{:S(2)}) copy-start(s32[8]{0:T(128)} %param.25) | copy-start | bytes 100
  44.9 26.5 %collective-permute-start = (bf16[256,16,128]{2,0,1:T(8,128)(2,1)}, bf16[256,16,128]{2,0,1:T(8,128)(2,1)}, u32[]{:S(2)}, u32[]{:S(2)}) collective-permute-start(bf16[256,16,128]{2,0,1:T(8,128)(2,1)} %get-tuple-element.587), channel_id=1, source_target_pairs={{0,8},{8,16},{16,24},{24,0},{1,9},{9,17},{17,25},{25,1},{2,10},{10... | collective-permute-start | bytes 3145736 | tf_op jit(solution)/shard_map/while/body/eval_jaxpr/ppermute | solution.py:32
  74.6 5.1 %copy-start.7 = (bf16[16,768,128]{2,1,0:T(8,128)(2,1)S(1)}, bf16[16,768,128]{2,1,0:T(8,128)(2,1)}, u32[]{:S(2)}) copy-start(bf16[16,768,128]{2,1,0:T(8,128)(2,1)} %get-tuple-element.613) | copy-start | bytes 9437188 | tf_op jit(solution)/shard_map/while
  88.3 23.7 %collective-permute-start = (bf16[256,16,128]{2,0,1:T(8,128)(2,1)}, bf16[256,16,128]{2,0,1:T(8,128)(2,1)}, u32[]{:S(2)}, u32[]{:S(2)}) collective-permute-start(bf16[256,16,128]{2,0,1:T(8,128)(2,1)} %get-tuple-element.587), channel_id=1, source_target_pairs={{0,8},{8,16},{16,24},{24,0},{1,9},{9,17},{17,25},{25,1},{2,10},{10... | collective-permute-start | bytes 3145736 | tf_op jit(solution)/shard_map/while/body/eval_jaxpr/ppermute | solution.py:32
  115.1 5.1 %copy-start.7 = (bf16[16,768,128]{2,1,0:T(8,128)(2,1)S(1)}, bf16[16,768,128]{2,1,0:T(8,128)(2,1)}, u32[]{:S(2)}) copy-start(bf16[16,768,128]{2,1,0:T(8,128)(2,1)} %get-tuple-element.613) | copy-start | bytes 9437188 | tf_op jit(solution)/shard_map/while
  128.8 22.7 %collective-permute-start = (bf16[256,16,128]{2,0,1:T(8,128)(2,1)}, bf16[256,16,128]{2,0,1:T(8,128)(2,1)}, u32[]{:S(2)}, u32[]{:S(2)}) collective-permute-start(bf16[256,16,128]{2,0,1:T(8,128)(2,1)} %get-tuple-element.587), channel_id=1, source_target_pairs={{0,8},{8,16},{16,24},{24,0},{1,9},{9,17},{17,25},{25,1},{2,10},{10... | collective-permute-start | bytes 3145736 | tf_op jit(solution)/shard_map/while/body/eval_jaxpr/ppermute | solution.py:32
  154.7 5.1 %copy-start.7 = (bf16[16,768,128]{2,1,0:T(8,128)(2,1)S(1)}, bf16[16,768,128]{2,1,0:T(8,128)(2,1)}, u32[]{:S(2)}) copy-start(bf16[16,768,128]{2,1,0:T(8,128)(2,1)} %get-tuple-element.613) | copy-start | bytes 9437188 | tf_op jit(solution)/shard_map/while
  168.3 9.8 %all-to-all-start = ((f32[4,16,256]{2,1,0:T(8,128)}), f32[4,16,256]{2,1,0:T(8,128)S(1)}, u32[]{:S(2)}, u32[]{:S(2)}) async-start(f32[4,16,256]{2,1,0:T(8,128)} %get-tuple-element.319), calls=%async_computation | async-start | bytes 131072 | tf_op jit(solution)/shard_map/all_to_all | solution.py:360
  178.1 6.1 %copy-start.2 = (bf16[256,8,128]{2,1,0:T(8,128)(2,1)S(1)}, bf16[256,8,128]{2,1,0:T(8,128)(2,1)}, u32[]{:S(2)}) copy-start(bf16[256,8,128]{2,1,0:T(8,128)(2,1)} %param.26) | copy-start | bytes 1572868
  178.1 94.3 %all-to-all-start.1 = ((f32[4,256,16,128]{3,1,2,0:T(8,128)}), f32[4,256,16,128]{3,1,2,0:T(8,128)}, u32[]{:S(2)}, u32[]{:S(2)}) async-start(f32[4,256,16,128]{3,1,2,0:T(8,128)} %convert_element_type.40), calls=%async_computation.1 | async-start | bytes 16777216 | tf_op jit(solution)/shard_map/all_to_all | solution.py:359
  184.2 3.6 %copy-start.3 = (bf16[256,8,128]{2,1,0:T(8,128)(2,1)S(1)}, bf16[256,8,128]{2,1,0:T(8,128)(2,1)}, u32[]{:S(2)}) copy-start(bf16[256,8,128]{2,1,0:T(8,128)(2,1)} %param.27) | copy-start | bytes 1572868
  191.5 1.2 copy-start.10
  282.2 51.3 %copy-start.1 = (bf16[8,768,128]{2,1,0:T(8,128)(2,1)S(1)}, bf16[8,768,128]{2,1,0:T(8,128)(2,1)}, u32[]{:S(2)}) copy-start(bf16[8,768,128]{2,1,0:T(8,128)(2,1)} %param.21) | copy-start | bytes 4718596

commit v2 on v1

--- a/solution.py
+++ b/solution.py
@@ -8,6 +8,7 @@
 from jax.sharding import PartitionSpec as P
 
 MESH = pl.DeviceIdType.MESH
+LOG2E = math.log2(math.e)
 
 SPAN = 128
 
@@ -256,6 +257,228 @@
     )(flat, out_weight)
 
 
+def gather_and_attend(queries, keys, values, meta, offsets, groups, fresh_keys, fresh_values):
+    heads_here, row_count, head_width = queries.shape
+    group_count, slot_count, _ = keys.shape
+    half = slot_count // 2
+    near = group_count // 2
+    spans_here = row_count // SPAN
+    factor = LOG2E / math.sqrt(head_width)
+
+    def kernel(
+        offsets_ref, groups_ref, q_ref, k_ref, v_ref, meta_ref, fk_ref, fv_ref, out_ref,
+        xf_k, xf_v, xs_k, xs_v, yf_k, yf_v, ys_k, ys_v, dn_k, dn_v, df_k, df_v,
+        meta_x, meta_y, meta_d, bias, top, total, mixed,
+        send, recv, meta_send, meta_recv,
+    ):
+        me = lax.axis_index("ctx")
+        head = lax.axis_index("head")
+        plane = head // 2
+        core = head % 2
+        parity = plane % 2
+        x_place = me + 1 - 2 * (me % 2)
+        y_place = (me + 2) % 4
+        d_place = 3 - me
+        to_x, to_y, to_d = {"ctx": x_place}, {"ctx": y_place}, {"ctx": d_place}
+        sibling = {"head": 2 * plane + 1 - core}
+        partner = {"head": head + 2 - 4 * parity}
+        barrier = pltpu.get_barrier_semaphore()
+        for device in (to_x, to_y, to_d, sibling, partner):
+            pl.semaphore_signal(barrier, inc=1, device_id=device, device_id_type=MESH)
+        pl.semaphore_wait(barrier, 5)
+
+        mine = pl.ds(core * near, near)
+        low = pl.ds(core * near, near // 2)
+        high = pl.ds(core * near + near // 2, near // 2)
+        first = pl.multiple_of(parity * half, 128)
+        second = pl.multiple_of((1 - parity) * half, 128)
+        started = []
+
+        def copy(source, target, device):
+            i = len(started)
+            made = pltpu.make_async_remote_copy(
+                src_ref=source, dst_ref=target, send_sem=send.at[i], recv_sem=recv.at[i],
+                device_id=device, device_id_type=MESH,
+            )
+            made.start()
+            started.append(made)
+            return made
+
+        meta_copies = []
+        for i, (target, device) in enumerate(((meta_x, to_x), (meta_y, to_y), (meta_d, to_d))):
+            made = pltpu.make_async_remote_copy(
+                src_ref=meta_ref, dst_ref=target, send_sem=meta_send.at[i], recv_sem=meta_recv.at[i],
+                device_id=device, device_id_type=MESH,
+            )
+            made.start()
+            meta_copies.append(made)
+
+        def own(ref, offset):
+            return ref.at[mine, pl.ds(offset, half)]
+
+        firsts = [
+            copy(own(ref, first), target.at[mine], device)
+            for ref, tx, ty in ((k_ref, xf_k, yf_k), (v_ref, xf_v, yf_v))
+            for target, device in ((tx, to_x), (ty, to_y))
+        ]
+
+        def fresh_head(h, carry):
+            g = groups_ref[h]
+            for t in range(spans_here):
+                span = pl.ds(t * SPAN, SPAN)
+                scores = lax.dot_general(
+                    q_ref[h, span], fk_ref[g, span], (((1,), (1,)), ((), ())),
+                    preferred_element_type=jnp.float32,
+                ) * factor
+                causal = lax.broadcasted_iota(jnp.int32, scores.shape, 0) >= lax.broadcasted_iota(
+                    jnp.int32, scores.shape, 1
+                )
+                scores = jnp.where(causal, scores, floor_score)
+                largest = jnp.max(scores, axis=1, keepdims=True)
+                expo = jnp.exp2(scores - largest)
+                top[h, span] = largest
+                total[h, span] = jnp.sum(expo, axis=1, keepdims=True)
+                mixed[h, span] = jnp.dot(
+                    expo.astype(jnp.bfloat16), fv_ref[g, span], preferred_element_type=jnp.float32
+                )
+            return carry
+
+        lax.fori_loop(0, heads_here, fresh_head, 0, unroll=2)
+        for made in meta_copies:
+            made.wait_recv()
+
+        places = ((me, meta_ref), (x_place, meta_x), (y_place, meta_y), (d_place, meta_d))
+        slot_ids = lax.broadcasted_iota(jnp.int32, (1, slot_count), 1)
+        lengths = [m[pl.ds(2 * group_count, 1), :].astype(jnp.int32) for _, m in places]
+        for b, (place, _) in enumerate(places):
+            start = jnp.zeros((1, slot_count), jnp.int32)
+            for (other, _), length in zip(places, lengths):
+                start = start + jnp.where(other < place, length, 0)
+            for t in range(spans_here):
+                limit = offsets_ref[me * spans_here + t]
+                visible = (slot_ids < lengths[b]) & (start + slot_ids < limit)
+                bias[b, pl.ds(t, 1), :] = jnp.where(visible, 0.0, floor_score)
+
+        def attend(b, offset, size, keys_of, values_of):
+            slots = pl.ds(offset, size)
+            meta_of = places[b][1]
+
+            def one(h, carry):
+                g = groups_ref[h]
+                key_rows, value_rows = keys_of(g), values_of(g)
+                key_scale = meta_of[pl.ds(g, 1), slots]
+                value_scale = meta_of[pl.ds(g + group_count, 1), slots]
+                raw = lax.dot_general(
+                    q_ref[h], key_rows, (((1,), (1,)), ((), ())), preferred_element_type=jnp.float32
+                )
+                for t in range(spans_here):
+                    span = pl.ds(t * SPAN, SPAN)
+                    scores = raw[t * SPAN:(t + 1) * SPAN] * key_scale + bias[b, pl.ds(t, 1), slots]
+                    before = top[h, span]
+                    largest = jnp.maximum(before, jnp.max(scores, axis=1, keepdims=True))
+                    keep = jnp.exp2(before - largest)
+                    expo = jnp.exp2(scores - largest)
+                    top[h, span] = largest
+                    total[h, span] = total[h, span] * keep + jnp.sum(expo, axis=1, keepdims=True)
+                    weights = (expo * value_scale).astype(jnp.bfloat16)
+                    mixed[h, span] = mixed[h, span] * keep + jnp.dot(
+                        weights, value_rows, preferred_element_type=jnp.float32
+                    )
+                return carry
+
+            lax.fori_loop(0, heads_here, one, 0, unroll=2)
+
+        def attend_ref(b, offset, k, v):
+            attend(b, offset, half, lambda g: k[g], lambda g: v[g])
+
+        attend(0, 0, slot_count, lambda g: k_ref[g], lambda g: v_ref[g])
+
+        def share(pairs):
+            return [copy(ref.at[part], ref.at[part], sibling) for ref, part in pairs]
+
+        def arrived(copies):
+            for made in copies:
+                made.wait_recv()
+
+        arrived(firsts)
+        relays = [
+            copy(source.at[part], target.at[part], device)
+            for source, target, part, device in (
+                (xf_k, dn_k, low, to_y), (yf_k, dn_k, high, to_x),
+                (xf_v, dn_v, low, to_y), (yf_v, dn_v, high, to_x),
+            )
+        ]
+        seconds = [
+            copy(own(ref, second), target.at[mine], device)
+            for ref, tx, ty in ((k_ref, xs_k, ys_k), (v_ref, xs_v, ys_v))
+            for target, device in ((tx, to_x), (ty, to_y))
+        ]
+        arrived(share([(xf_k, mine), (xf_v, mine), (yf_k, mine), (yf_v, mine)]))
+        attend_ref(1, first, xf_k, xf_v)
+        arrived(relays)
+        across = [
+            copy(source.at[part], target.at[part], partner)
+            for source, target in ((dn_k, df_k), (dn_v, df_v))
+            for part in (low, high)
+        ]
+        near_shared = share([(dn_k, mine), (dn_v, mine)])
+        attend_ref(2, first, yf_k, yf_v)
+        arrived(near_shared)
+        attend_ref(3, first, dn_k, dn_v)
+        arrived(seconds)
+        second_shared = share([(xs_k, mine), (xs_v, mine), (ys_k, mine), (ys_v, mine)])
+        arrived(across)
+        far_shared = share([(df_k, mine), (df_v, mine)])
+        arrived(second_shared)
+        attend_ref(1, second, xs_k, xs_v)
+        attend_ref(2, second, ys_k, ys_v)
+        arrived(far_shared)
+        attend_ref(3, second, df_k, df_v)
+
+        def finish(h, carry):
+            columns = pl.ds(pl.multiple_of(h * head_width, head_width), head_width)
+            out_ref[:, columns] = (mixed[h] / total[h]).astype(jnp.bfloat16)
+            return carry
+
+        lax.fori_loop(0, heads_here, finish, 0)
+        for made in started + meta_copies:
+            made.wait_send()
+
+    chunk = pltpu.VMEM((group_count, half, head_width), jnp.bfloat16)
+    table = pltpu.VMEM(meta.shape, jnp.float32)
+    dma = pltpu.SemaphoreType.DMA
+    copies = 4 + 4 + 4 + 4 + 4 + 2 + 4 + 2
+    whole = pl.BlockSpec(memory_space=pltpu.VMEM)
+    scalar = pl.BlockSpec(memory_space=pltpu.SMEM)
+    return pl.pallas_call(
+        kernel,
+        out_shape=jax.ShapeDtypeStruct((row_count, heads_here * head_width), jnp.bfloat16),
+        in_specs=[scalar, scalar] + [whole] * 6,
+        out_specs=whole,
+        scratch_shapes=[chunk] * 12
+        + [table] * 3
+        + [
+            pltpu.VMEM((4, 8, slot_count), jnp.float32),
+            pltpu.VMEM((heads_here, row_count, 1), jnp.float32),
+            pltpu.VMEM((heads_here, row_count, 1), jnp.float32),
+            pltpu.VMEM((heads_here, row_count, head_width), jnp.float32),
+            dma((copies,)),
+            dma((copies,)),
+            dma((3,)),
+            dma((3,)),
+        ],
+        compiler_params=pltpu.CompilerParams(
+            collective_id=2, has_side_effects=True, vmem_limit_bytes=56 * 1024 * 1024
+        ),
+        cost_estimate=pl.CostEstimate(
+            flops=16 * row_count * heads_here * slot_count * head_width,
+            bytes_accessed=8 * group_count * slot_count * head_width,
+            transcendentals=4 * row_count * heads_here * slot_count,
+        ),
+        name="gather_and_attend",
+    )(offsets, groups, queries, keys, values, meta, fresh_keys, fresh_values)
+
+
 def shards(
     queries,
     cache_keys,
@@ -276,7 +499,35 @@
     spans_here = row_count // SPAN
     inverse = 1.0 / math.sqrt(head_width)
     codes = jnp.arange(scale_table.shape[1], dtype=jnp.int32)
-    one_hot = (scale_index[:, :, None] == codes[None, None, :]).astype(jnp.float32)
+    one_hot = scale_index[:, :, None] == codes[None, None, :]
+    if ctx_count == 4 and lax.axis_size("head") % 4 == 0:
+        expanded = jnp.repeat(
+            jnp.sum(
+                jnp.where(one_hot[None], scale_table[:, None, None, :], 0.0), axis=3
+            ),
+            slot_count // scale_index.shape[1],
+            axis=2,
+        )
+        meta = jnp.concatenate(
+            [
+                expanded[0] * (inverse * LOG2E),
+                expanded[1],
+                jnp.broadcast_to(hist_lengths.astype(jnp.float32)[:, None], (8, slot_count)),
+            ],
+            axis=0,
+        )
+        flat = gather_and_attend(
+            jnp.transpose(queries, (1, 0, 2)),
+            cache_keys,
+            cache_values,
+            meta,
+            span_offsets,
+            head_groups,
+            jnp.transpose(new_keys, (1, 0, 2)),
+            jnp.transpose(new_values, (1, 0, 2)),
+        )
+        return project_and_reduce(flat, out_weight)
+    one_hot = one_hot.astype(jnp.float32)
     block_scales = jnp.einsum("kbn,tn->tkb", one_hot, scale_table, precision=lax.Precision.HIGHEST)
     slot_scales = jnp.repeat(block_scales, slot_count // scale_index.shape[1], axis=2)
     head_scales = jnp.take(slot_scales, head_groups, axis=1)

time: 338 us -> 150 us (0.44)
  the two profiles are of different devices: /device:TPU:8 before, /device:TPU:0 now
where the time goes in v2:
time: 150 us
  Pallas kernels  141 us (94%)
  local copies, waits for them, and re-layouts  6.46 us (4%)
  other arithmetic  1.56 us (1%)
    pallas_call x1, Pallas kernels, gather_and_attend(): pl.pallas_call(kernel, out_shape=jax.ShapeDtypeStruct((row_count, heads_h...  86.6 us
    pallas_call x1, Pallas kernels, project_and_reduce(): pl.pallas_call(kernel, out_shape=jax.ShapeDtypeStruct((rows, width), jnp....  54.1 us
    unnamed x7, local copies, waits for them, and re-layouts  5.16 us

profile of v2, /device:TPU:0, one launch (start us, length us, event | category | flops | bytes accessed | tf_op | source)
XLA Modules:
  0.0 149.5 jit_solution(637877801135741996)
XLA Ops:
  0.0 0.0 copy-start
  0.0 0.0 copy-start.1
  0.8 0.1 pad.2.clone
  0.8 0.8 copy.18
  1.6 0.1 iota_compare_fusion
  1.7 0.8 select_reduce_fusion
  2.5 0.1 broadcast_bitcast_fusion
  2.5 0.7 maximum_maximum_fusion.meta_ref
  3.2 2.5 %copy.30 = bf16[256,16,128]{2,0,1:T(8,128)(2,1)} copy(bf16[256,16,128]{2,1,0:T(8,128)(2,1)} %param.11) | data formatting | bytes 2097152 | tf_op args[0]
  5.8 0.0 copy-done
  5.8 0.0 copy-done.1
  5.8 1.1 copy_bitcast_fusion.1
  6.9 86.6 %gather_and_attend.1.flat_ref = bf16[256,2048]{1,0:T(8,128)(2,1)} custom-call(s32[8]{0:T(128)} %offsets_ref.1, s32[16]{0:T(128)} %groups_ref.1, bf16[16,256,128]{2,1,0:T(8,128)(2,1)} %bitcast.16, bf16[8,768,128]{2,1,0:T(8,128)(2,1)} %k_ref.1, bf16[8,768,128]{2,1,0:T(8,128)(2,1)} %v_ref.1, f32[24,768]{1,0:T(8,128)} %maximum_maximum_fusion.meta_ref, ...), custom_call_target="tpu_custom_call" | custom-call | flops 6442450944 | bytes 6291456 | tf_op jit(solution)/shard_map/gather_and_attend/pallas_call | solution.py:453
  93.5 54.1 %project_and_reduce.1 = bf16[256,1024]{1,0:T(8,128)(2,1)} custom-call(bf16[256,2048]{1,0:T(8,128)(2,1)} %gather_and_attend.1.flat_ref, bf16[2048,8192]{1,0:T(8,128)(2,1)} %weight_ref.1), custom_call_target="tpu_custom_call" | custom-call | flops 8589934592 | bytes 33554432 | tf_op jit(solution)/shard_map/project_and_reduce/pallas_call | solution.py:226
  147.6 1.9 %copy.33 = bf16[256,1024]{1,0:T(8,128)(2,1)} copy(bf16[256,1024]{1,0:T(8,128)(2,1)} %project_and_reduce.1) | data formatting | bytes 1048576
  (2 shorter events, 0.0 us)
Async XLA Ops:
  0.0 5.8 %copy-start = (bf16[256,8,128]{2,1,0:T(8,128)(2,1)S(1)}, bf16[256,8,128]{2,1,0:T(8,128)(2,1)}, u32[]{:S(2)}) copy-start(bf16[256,8,128]{2,1,0:T(8,128)(2,1)} %param.19) | copy-start | bytes 1572868
  0.0 5.8 %copy-start.1 = (bf16[256,8,128]{2,1,0:T(8,128)(2,1)S(1)}, bf16[256,8,128]{2,1,0:T(8,128)(2,1)}, u32[]{:S(2)}) copy-start(bf16[256,8,128]{2,1,0:T(8,128)(2,1)} %param.18) | copy-start | bytes 1572868

commit v3 on v2

--- a/solution.py
+++ b/solution.py
@@ -202,9 +202,7 @@
             multiply(2 * step, to_pair)
             to_sibling(d).start()
             multiply(2 * step + 1, to_own)
-            if step > 0:
-                combine(targets[step - 1])
-        combine(targets[planes - 1])
+            combine(d)
 
         for step in range(planes):
             d = targets[step]
@@ -314,7 +312,8 @@
             meta_copies.append(made)
 
         def own(ref, offset):
-            return ref.at[mine, pl.ds(offset, half)]
+            slots = pl.ds(offset, half)
+            return ref.at[mine, slots] if ref is k_ref else ref.at[mine, :, slots]
 
         firsts = [
             copy(own(ref, first), target.at[mine], device)
@@ -327,19 +326,20 @@
             for t in range(spans_here):
                 span = pl.ds(t * SPAN, SPAN)
                 scores = lax.dot_general(
-                    q_ref[h, span], fk_ref[g, span], (((1,), (1,)), ((), ())),
+                    fk_ref[g, span], q_ref[h, span], (((1,), (1,)), ((), ())),
                     preferred_element_type=jnp.float32,
                 ) * factor
-                causal = lax.broadcasted_iota(jnp.int32, scores.shape, 0) >= lax.broadcasted_iota(
-                    jnp.int32, scores.shape, 1
+                causal = lax.broadcasted_iota(jnp.int32, scores.shape, 1) >= lax.broadcasted_iota(
+                    jnp.int32, scores.shape, 0
                 )
                 scores = jnp.where(causal, scores, floor_score)
-                largest = jnp.max(scores, axis=1, keepdims=True)
+                largest = jnp.max(scores, axis=0, keepdims=True)
                 expo = jnp.exp2(scores - largest)
-                top[h, span] = largest
-                total[h, span] = jnp.sum(expo, axis=1, keepdims=True)
-                mixed[h, span] = jnp.dot(
-                    expo.astype(jnp.bfloat16), fv_ref[g, span], preferred_element_type=jnp.float32
+                top[h, :, span] = largest
+                total[h, :, span] = jnp.sum(expo, axis=0, keepdims=True)
+                mixed[h, :, span] = jnp.dot(
+                    fv_ref[g, :, span], expo.astype(jnp.bfloat16),
+                    preferred_element_type=jnp.float32,
                 )
             return carry
 
@@ -348,42 +348,53 @@
             made.wait_recv()
 
         places = ((me, meta_ref), (x_place, meta_x), (y_place, meta_y), (d_place, meta_d))
-        slot_ids = lax.broadcasted_iota(jnp.int32, (1, slot_count), 1)
-        lengths = [m[pl.ds(2 * group_count, 1), :].astype(jnp.int32) for _, m in places]
+        slot_ids = lax.broadcasted_iota(jnp.int32, (slot_count, SPAN), 0)
+        lengths = [
+            m[2 * group_count, :, pl.ds(0, SPAN)].astype(jnp.int32) for _, m in places
+        ]
         for b, (place, _) in enumerate(places):
-            start = jnp.zeros((1, slot_count), jnp.int32)
+            start = jnp.zeros((1, SPAN), jnp.int32)
             for (other, _), length in zip(places, lengths):
                 start = start + jnp.where(other < place, length, 0)
             for t in range(spans_here):
-                limit = offsets_ref[me * spans_here + t]
-                visible = (slot_ids < lengths[b]) & (start + slot_ids < limit)
-                bias[b, pl.ds(t, 1), :] = jnp.where(visible, 0.0, floor_score)
+                limit = jnp.minimum(lengths[b], offsets_ref[me * spans_here + t] - start)
+                bias[b, :, pl.ds(t * SPAN, SPAN)] = jnp.where(slot_ids < limit, 0.0, floor_score)
 
         def attend(b, offset, size, keys_of, values_of):
-            slots = pl.ds(offset, size)
             meta_of = places[b][1]
+
+            def scales(row, j):
+                part = meta_of[row, :, pl.ds(offset + j * SPAN, SPAN)]
+                return jnp.concatenate([part] * spans_here, axis=1)
 
             def one(h, carry):
                 g = groups_ref[h]
-                key_rows, value_rows = keys_of(g), values_of(g)
-                key_scale = meta_of[pl.ds(g, 1), slots]
-                value_scale = meta_of[pl.ds(g + group_count, 1), slots]
                 raw = lax.dot_general(
-                    q_ref[h], key_rows, (((1,), (1,)), ((), ())), preferred_element_type=jnp.float32
+                    keys_of(g), q_ref[h], (((1,), (1,)), ((), ())),
+                    preferred_element_type=jnp.float32,
                 )
-                for t in range(spans_here):
-                    span = pl.ds(t * SPAN, SPAN)
-                    scores = raw[t * SPAN:(t + 1) * SPAN] * key_scale + bias[b, pl.ds(t, 1), slots]
-                    before = top[h, span]
-                    largest = jnp.maximum(before, jnp.max(scores, axis=1, keepdims=True))
-                    keep = jnp.exp2(before - largest)
-                    expo = jnp.exp2(scores - largest)
-                    top[h, span] = largest
-                    total[h, span] = total[h, span] * keep + jnp.sum(expo, axis=1, keepdims=True)
-                    weights = (expo * value_scale).astype(jnp.bfloat16)
-                    mixed[h, span] = mixed[h, span] * keep + jnp.dot(
-                        weights, value_rows, preferred_element_type=jnp.float32
-                    )
+                scores = [
+                    raw[j * SPAN:(j + 1) * SPAN] * scales(g, j)
+                    + bias[b, pl.ds(offset + j * SPAN, SPAN), :]
+                    for j in range(size // SPAN)
+                ]
+                before = top[h]
+                largest = before
+                for score in scores:
+                    largest = jnp.maximum(largest, jnp.max(score, axis=0, keepdims=True))
+                keep = jnp.exp2(before - largest)
+                added = total[h] * keep
+                weights = []
+                for j, score in enumerate(scores):
+                    expo = jnp.exp2(score - largest)
+                    added = added + jnp.sum(expo, axis=0, keepdims=True)
+                    weights.append((expo * scales(g + group_count, j)).astype(jnp.bfloat16))
+                top[h] = largest
+                total[h] = added
+                mixed[h] = mixed[h] * keep + jnp.dot(
+                    values_of(g), jnp.concatenate(weights, axis=0),
+                    preferred_element_type=jnp.float32,
+                )
                 return carry
 
             lax.fori_loop(0, heads_here, one, 0, unroll=2)
@@ -437,14 +448,15 @@
 
         def finish(h, carry):
             columns = pl.ds(pl.multiple_of(h * head_width, head_width), head_width)
-            out_ref[:, columns] = (mixed[h] / total[h]).astype(jnp.bfloat16)
+            out_ref[:, columns] = jnp.transpose(mixed[h] / total[h]).astype(jnp.bfloat16)
             return carry
 
         lax.fori_loop(0, heads_here, finish, 0)
         for made in started + meta_copies:
             made.wait_send()
 
-    chunk = pltpu.VMEM((group_count, half, head_width), jnp.bfloat16)
+    key_chunk = pltpu.VMEM((group_count, half, head_width), jnp.bfloat16)
+    value_chunk = pltpu.VMEM((group_count, head_width, half), jnp.bfloat16)
     table = pltpu.VMEM(meta.shape, jnp.float32)
     dma = pltpu.SemaphoreType.DMA
     copies = 4 + 4 + 4 + 4 + 4 + 2 + 4 + 2
@@ -455,13 +467,13 @@
         out_shape=jax.ShapeDtypeStruct((row_count, heads_here * head_width), jnp.bfloat16),
         in_specs=[scalar, scalar] + [whole] * 6,
         out_specs=whole,
-        scratch_shapes=[chunk] * 12
+        scratch_shapes=[key_chunk, value_chunk] * 6
         + [table] * 3
         + [
-            pltpu.VMEM((4, 8, slot_count), jnp.float32),
-            pltpu.VMEM((heads_here, row_count, 1), jnp.float32),
-            pltpu.VMEM((heads_here, row_count, 1), jnp.float32),
-            pltpu.VMEM((heads_here, row_count, head_width), jnp.float32),
+            pltpu.VMEM((4, slot_count, row_count), jnp.float32),
+            pltpu.VMEM((heads_here, 1, row_count), jnp.float32),
+            pltpu.VMEM((heads_here, 1, row_count), jnp.float32),
+            pltpu.VMEM((heads_here, head_width, row_count), jnp.float32),
             dma((copies,)),
             dma((copies,)),
             dma((3,)),
@@ -519,12 +531,12 @@
         flat = gather_and_attend(
             jnp.transpose(queries, (1, 0, 2)),
             cache_keys,
-            cache_values,
-            meta,
+            jnp.transpose(cache_values, (0, 2, 1)),
+            meta[:, None, :],
             span_offsets,
             head_groups,
             jnp.transpose(new_keys, (1, 0, 2)),
-            jnp.transpose(new_values, (1, 0, 2)),
+            jnp.transpose(new_values, (1, 2, 0)),
         )
         return project_and_reduce(flat, out_weight)
     one_hot = one_hot.astype(jnp.float32)

time: 150 us -> 144 us (0.960)
  Pallas kernels: 141 us -> 132 us
  local copies, waits for them, and re-layouts: 6.46 us -> 9.36 us
    pallas_call x1, Pallas kernels: 86.6 us -> 81.1 us  [gather_and_attend(): pl.pallas_call(kernel, out_shape=jax.ShapeDtypeStruct((row_count, heads_h...]
    unnamed x7 -> x12, local copies, waits for them, and re-layouts: 5.16 us -> 8.54 us
    pallas_call x1, Pallas kernels: 54.1 us -> 51.2 us  [project_and_reduce(): pl.pallas_call(kernel, out_shape=jax.ShapeDtypeStruct((rows, width), jnp....]
where the time goes in v3:
time: 144 us; the launch traced here: 143 us
  Pallas kernels  132 us (92%)
  local copies, waits for them, and re-layouts  9.36 us (6%)
    pallas_call x1, Pallas kernels, gather_and_attend(): pl.pallas_call(kernel, out_shape=jax.ShapeDtypeStruct((row_count, heads_h...  81.1 us
    pallas_call x1, Pallas kernels, project_and_reduce(): pl.pallas_call(kernel, out_shape=jax.ShapeDtypeStruct((rows, width), jnp....  51.2 us
    unnamed x12, local copies, waits for them, and re-layouts  8.54 us

profile of v3, /device:TPU:0, one launch (start us, length us, event | category | flops | bytes accessed | tf_op | source)
XLA Modules:
  0.0 143.4 jit_solution(15462906955620003137)
XLA Ops:
  0.0 0.0 copy-start.2
  0.0 0.0 copy-start.1
  0.8 0.1 pad.2.clone
  0.9 0.8 copy.20
  1.6 0.1 iota_compare_fusion
  1.7 0.8 select_reduce_fusion
  2.5 0.1 broadcast_bitcast_fusion
  2.6 0.1 maximum_maximum_fusion
  2.6 0.7 broadcast_in_dim.50.meta_ref
  3.3 1.9 %copy.32 = bf16[256,8,128]{2,0,1:T(8,128)(2,1)} copy(bf16[256,8,128]{2,1,0:T(8,128)(2,1)} %param.18) | data formatting | bytes 1048576 | tf_op args[7]
  5.2 0.0 copy-done.2
  5.2 0.0 copy-start
  5.2 1.1 copy.26
  6.4 0.0 copy-done.1
  6.4 1.3 copy.31
  7.6 0.0 copy-done
  7.6 1.6 %copy.19 = bf16[8,768,128]{1,2,0:T(8,128)(2,1)} copy(bf16[8,768,128]{2,1,0:T(8,128)(2,1)S(1)} %copy-done) | data formatting | bytes 3145728 | tf_op args[2]
  9.2 81.1 %gather_and_attend.1.flat_ref = bf16[256,2048]{1,0:T(8,128)(2,1)} custom-call(s32[8]{0:T(128)} %offsets_ref.1, s32[16]{0:T(128)} %groups_ref.1, bf16[16,256,128]{2,1,0:T(8,128)(2,1)} %bitcast.18, bf16[8,768,128]{2,1,0:T(8,128)(2,1)} %k_ref.1, bf16[8,128,768]{2,1,0:T(8,128)(2,1)} %bitcast.17, f32[24,1,768]{2,1,0:T(1,128)} %broadcast_in_dim.50.meta_ref, ...), custom_call_target="tpu_custom_call" | custom-call | flops 6442450944 | bytes 6291456 | tf_op jit(solution)/shard_map/gather_and_attend/pallas_call | solution.py:465
  90.4 51.2 %project_and_reduce.1 = bf16[256,1024]{1,0:T(8,128)(2,1)} custom-call(bf16[256,2048]{1,0:T(8,128)(2,1)} %gather_and_attend.1.flat_ref, bf16[2048,8192]{1,0:T(8,128)(2,1)} %weight_ref.1), custom_call_target="tpu_custom_call" | custom-call | flops 8589934592 | bytes 33554432 | tf_op jit(solution)/shard_map/project_and_reduce/pallas_call | solution.py:224
  141.5 1.9 %copy.35 = bf16[256,1024]{1,0:T(8,128)(2,1)} copy(bf16[256,1024]{1,0:T(8,128)(2,1)} %project_and_reduce.1) | data formatting | bytes 1048576
  (2 shorter events, 0.0 us)
Async XLA Ops:
  0.0 5.2 %copy-start.2 = (bf16[256,8,128]{2,1,0:T(8,128)(2,1)S(1)}, bf16[256,8,128]{2,1,0:T(8,128)(2,1)}, u32[]{:S(2)}) copy-start(bf16[256,8,128]{2,1,0:T(8,128)(2,1)} %param.19) | copy-start | bytes 1572868
  0.0 6.4 %copy-start.1 = (bf16[256,16,128]{2,1,0:T(8,128)(2,1)S(1)}, bf16[256,16,128]{2,1,0:T(8,128)(2,1)}, u32[]{:S(2)}) copy-start(bf16[256,16,128]{2,1,0:T(8,128)(2,1)} %param.11) | copy-start | bytes 3145732
  5.2 2.4 %copy-start = (bf16[8,768,128]{2,1,0:T(8,128)(2,1)S(1)}, bf16[8,768,128]{2,1,0:T(8,128)(2,1)}, u32[]{:S(2)}) copy-start(bf16[8,768,128]{2,1,0:T(8,128)(2,1)} %param.13) | copy-start | bytes 4718596

commit v4 on v3

--- a/solution.py
+++ b/solution.py
@@ -42,12 +42,13 @@
     planes = heads // 2
     rows, depth = flat.shape
     width = out_weight.shape[1] // heads
-    pieces = 4
+    pieces = 8
+    flying = 4
     piece = rows // pieces
     tile = 256
     slots = 4
     order = [
-        sorted(range(planes), key=lambda d, z=z: (-abs(d - z), -d if z < planes // 2 else d))
+        sorted(range(planes), key=lambda d, z=z: (-abs(d - z), d if z < planes // 2 else -d))
         for z in range(planes)
     ]
 
@@ -155,6 +156,14 @@
                     def _():
                         up_out[d, p] = total.astype(jnp.bfloat16)
 
+                    @pl.when(p >= flying)
+                    def _():
+                        upward(d, p - flying).wait_send()
+
+                    @pl.when((p < flying) & (d < planes - 1))
+                    def _():
+                        upward(d + 1, p + pieces - flying).wait_send()
+
                     upward(d, p).start()
 
                 @pl.when(d < plane)
@@ -172,6 +181,14 @@
                     def _():
                         down_out[d, p] = total.astype(jnp.bfloat16)
 
+                    @pl.when(p >= flying)
+                    def _():
+                        downward(d, p - flying).wait_send()
+
+                    @pl.when((p < flying) & (d > 0))
+                    def _():
+                        downward(d - 1, p + pieces - flying).wait_send()
+
                     downward(d, p).start()
 
                 @pl.when(d == plane)
@@ -204,19 +221,18 @@
             multiply(2 * step + 1, to_own)
             combine(d)
 
-        for step in range(planes):
-            d = targets[step]
+        for d in targets:
             to_sibling(d).wait_send()
 
-            @pl.loop(0, pieces)
-            def _(p, d=d):
-                @pl.when(d > plane)
-                def _():
-                    upward(d, p).wait_send()
-
-                @pl.when(d < plane)
-                def _():
-                    downward(d, p).wait_send()
+        @pl.loop(pieces - flying, pieces)
+        def _(p):
+            @pl.when(has_above)
+            def _():
+                upward(plane + 1, p).wait_send()
+
+            @pl.when(has_below)
+            def _():
+                downward(plane - 1, p).wait_send()
 
     block = (planes, rows, width)
     cut = (planes, pieces, piece, width)
@@ -419,13 +435,13 @@
                 (xf_v, dn_v, low, to_y), (yf_v, dn_v, high, to_x),
             )
         ]
+        arrived(share([(xf_k, mine), (xf_v, mine), (yf_k, mine), (yf_v, mine)]))
+        attend_ref(1, first, xf_k, xf_v)
         seconds = [
             copy(own(ref, second), target.at[mine], device)
             for ref, tx, ty in ((k_ref, xs_k, ys_k), (v_ref, xs_v, ys_v))
             for target, device in ((tx, to_x), (ty, to_y))
         ]
-        arrived(share([(xf_k, mine), (xf_v, mine), (yf_k, mine), (yf_v, mine)]))
-        attend_ref(1, first, xf_k, xf_v)
         arrived(relays)
         across = [
             copy(source.at[part], target.at[part], partner)
@@ -438,10 +454,10 @@
         attend_ref(3, first, dn_k, dn_v)
         arrived(seconds)
         second_shared = share([(xs_k, mine), (xs_v, mine), (ys_k, mine), (ys_v, mine)])
+        arrived(second_shared)
+        attend_ref(1, second, xs_k, xs_v)
         arrived(across)
         far_shared = share([(df_k, mine), (df_v, mine)])
-        arrived(second_shared)
-        attend_ref(1, second, xs_k, xs_v)
         attend_ref(2, second, ys_k, ys_v)
         arrived(far_shared)
         attend_ref(3, second, df_k, df_v)

time: 144 us -> 145 us (level)
  the two profiles are of different devices: /device:TPU:0 before, /device:TPU:8 now
where the time goes in v4:
time: 145 us; the launch traced here: 144 us
  Pallas kernels  133 us (92%)
  local copies, waits for them, and re-layouts  9.36 us (6%)
    pallas_call x1, Pallas kernels, gather_and_attend(): pl.pallas_call(kernel, out_shape=jax.ShapeDtypeStruct((row_count, heads_h...  81.7 us
    pallas_call x1, Pallas kernels, project_and_reduce(): pl.pallas_call(kernel, out_shape=jax.ShapeDtypeStruct((rows, width), jnp....  51.6 us
    unnamed x12, local copies, waits for them, and re-layouts  8.54 us

profile of v4, /device:TPU:8, one launch (start us, length us, event | category | flops | bytes accessed | tf_op | source)
XLA Modules:
  0.0 144.4 jit_solution(11408469880052222198)
XLA Ops:
  0.0 0.0 copy-start.2
  0.0 0.0 copy-start.1
  0.8 0.1 pad.2.clone
  0.9 0.8 copy.20
  1.6 0.1 iota_compare_fusion
  1.7 0.8 select_reduce_fusion
  2.5 0.1 broadcast_bitcast_fusion
  2.6 0.1 maximum_maximum_fusion
  2.6 0.7 broadcast_in_dim.50.meta_ref
  3.3 1.9 %copy.32 = bf16[256,8,128]{2,0,1:T(8,128)(2,1)} copy(bf16[256,8,128]{2,1,0:T(8,128)(2,1)} %param.18) | data formatting | bytes 1048576 | tf_op args[7]
  5.2 0.0 copy-done.2
  5.2 0.0 copy-start
  5.2 1.1 copy.26
  6.4 0.0 copy-done.1
  6.4 1.3 copy.31
  7.6 0.0 copy-done
  7.6 1.6 %copy.19 = bf16[8,768,128]{1,2,0:T(8,128)(2,1)} copy(bf16[8,768,128]{2,1,0:T(8,128)(2,1)S(1)} %copy-done) | data formatting | bytes 3145728 | tf_op args[2]
  9.2 81.7 %gather_and_attend.1.flat_ref = bf16[256,2048]{1,0:T(8,128)(2,1)} custom-call(s32[8]{0:T(128)} %offsets_ref.1, s32[16]{0:T(128)} %groups_ref.1, bf16[16,256,128]{2,1,0:T(8,128)(2,1)} %bitcast.18, bf16[8,768,128]{2,1,0:T(8,128)(2,1)} %k_ref.1, bf16[8,128,768]{2,1,0:T(8,128)(2,1)} %bitcast.17, f32[24,1,768]{2,1,0:T(1,128)} %broadcast_in_dim.50.meta_ref, ...), custom_call_target="tpu_custom_call" | custom-call | flops 6442450944 | bytes 6291456 | tf_op jit(solution)/shard_map/gather_and_attend/pallas_call | solution.py:481
  90.9 51.6 %project_and_reduce.1 = bf16[256,1024]{1,0:T(8,128)(2,1)} custom-call(bf16[256,2048]{1,0:T(8,128)(2,1)} %gather_and_attend.1.flat_ref, bf16[2048,8192]{1,0:T(8,128)(2,1)} %weight_ref.1), custom_call_target="tpu_custom_call" | custom-call | flops 8589934592 | bytes 33554432 | tf_op jit(solution)/shard_map/project_and_reduce/pallas_call | solution.py:240
  142.5 1.9 %copy.35 = bf16[256,1024]{1,0:T(8,128)(2,1)} copy(bf16[256,1024]{1,0:T(8,128)(2,1)} %project_and_reduce.1) | data formatting | bytes 1048576
  (2 shorter events, 0.0 us)
Async XLA Ops:
  0.0 5.2 %copy-start.2 = (bf16[256,8,128]{2,1,0:T(8,128)(2,1)S(1)}, bf16[256,8,128]{2,1,0:T(8,128)(2,1)}, u32[]{:S(2)}) copy-start(bf16[256,8,128]{2,1,0:T(8,128)(2,1)} %param.19) | copy-start | bytes 1572868
  0.0 6.4 %copy-start.1 = (bf16[256,16,128]{2,1,0:T(8,128)(2,1)S(1)}, bf16[256,16,128]{2,1,0:T(8,128)(2,1)}, u32[]{:S(2)}) copy-start(bf16[256,16,128]{2,1,0:T(8,128)(2,1)} %param.11) | copy-start | bytes 3145732
  5.2 2.4 %copy-start = (bf16[8,768,128]{2,1,0:T(8,128)(2,1)S(1)}, bf16[8,768,128]{2,1,0:T(8,128)(2,1)}, u32[]{:S(2)}) copy-start(bf16[8,768,128]{2,1,0:T(8,128)(2,1)} %param.13) | copy-start | bytes 4718596

commit v5 on v4

--- a/solution.py
+++ b/solution.py
@@ -73,6 +73,7 @@
             return d
 
         targets = [target(step) for step in range(planes)]
+        both_ways = (targets[0] > plane) != (targets[min(1, planes - 1)] > plane)
         blocks = []
         for d in targets:
             blocks += [2 * d + 1 - core, 2 * d + core]
@@ -136,11 +137,10 @@
                     ),
                 )
 
-        def combine(d):
-            to_sibling(d).wait_recv()
-
-            @pl.loop(0, pieces)
-            def _(p):
+        def combine(begin, end, place_of):
+            @pl.loop(begin, end)
+            def _(i):
+                d, p = place_of(i)
                 span = pl.ds(pl.multiple_of(p * piece, piece), piece)
 
                 @pl.when(d > plane)
@@ -219,7 +219,21 @@
             multiply(2 * step, to_pair)
             to_sibling(d).start()
             multiply(2 * step + 1, to_own)
-            combine(d)
+            to_sibling(d).wait_recv()
+            if planes < 2 or step > 1:
+                combine(0, pieces, lambda i, d=d: (d, i))
+            elif step == 0:
+                early = jnp.where(both_ways, 0, flying)
+                combine(0, early, lambda i, d=d: (d, i))
+            else:
+                before = targets[0]
+
+                def in_turn(i, d=d):
+                    later = jnp.where(both_ways, i % 2, i // pieces)
+                    p = jnp.where(both_ways, i // 2, i % pieces)
+                    return jnp.where(later == 1, d, before), p
+
+                combine(early, 2 * pieces, in_turn)
 
         for d in targets:
             to_sibling(d).wait_send()
@@ -418,7 +432,11 @@
         def attend_ref(b, offset, k, v):
             attend(b, offset, half, lambda g: k[g], lambda g: v[g])
 
-        attend(0, 0, slot_count, lambda g: k_ref[g], lambda g: v_ref[g])
+        def attend_own(offset):
+            slots = pl.ds(offset, half)
+            attend(0, offset, half, lambda g: k_ref[g, slots], lambda g: v_ref[g, :, slots])
+
+        attend_own(0)
 
         def share(pairs):
             return [copy(ref.at[part], ref.at[part], sibling) for ref, part in pairs]
@@ -435,8 +453,8 @@
                 (xf_v, dn_v, low, to_y), (yf_v, dn_v, high, to_x),
             )
         ]
-        arrived(share([(xf_k, mine), (xf_v, mine), (yf_k, mine), (yf_v, mine)]))
-        attend_ref(1, first, xf_k, xf_v)
+        first_shared = share([(xf_k, mine), (xf_v, mine), (yf_k, mine), (yf_v, mine)])
+        attend_own(half)
         seconds = [
             copy(own(ref, second), target.at[mine], device)
             for ref, tx, ty in ((k_ref, xs_k, ys_k), (v_ref, xs_v, ys_v))
@@ -449,15 +467,17 @@
             for part in (low, high)
         ]
         near_shared = share([(dn_k, mine), (dn_v, mine)])
+        arrived(first_shared)
+        attend_ref(1, first, xf_k, xf_v)
         attend_ref(2, first, yf_k, yf_v)
+        arrived(seconds)
+        second_shared = share([(xs_k, mine), (xs_v, mine), (ys_k, mine), (ys_v, mine)])
         arrived(near_shared)
         attend_ref(3, first, dn_k, dn_v)
-        arrived(seconds)
-        second_shared = share([(xs_k, mine), (xs_v, mine), (ys_k, mine), (ys_v, mine)])
+        arrived(across)
+        far_shared = share([(df_k, mine), (df_v, mine)])
         arrived(second_shared)
         attend_ref(1, second, xs_k, xs_v)
-        arrived(across)
-        far_shared = share([(df_k, mine), (df_v, mine)])
         attend_ref(2, second, ys_k, ys_v)
         arrived(far_shared)
         attend_ref(3, second, df_k, df_v)

time: 145 us -> 154 us (1.062)
  Pallas kernels: 133 us -> 143 us
    pallas_call x1, Pallas kernels: 51.6 us -> 58.9 us  [project_and_reduce(): pl.pallas_call(kernel, out_shape=jax.ShapeDtypeStruct((rows, width), jnp....]
    pallas_call x1, Pallas kernels: 81.7 us -> 83.8 us  [gather_and_attend(): pl.pallas_call(kernel, out_shape=jax.ShapeDtypeStruct((row_count, heads_h...]
where the time goes in v5:
time: 154 us
  Pallas kernels  143 us (93%)
  local copies, waits for them, and re-layouts  9.36 us (6%)
    pallas_call x1, Pallas kernels, gather_and_attend(): pl.pallas_call(kernel, out_shape=jax.ShapeDtypeStruct((row_count, heads_h...  83.8 us
    pallas_call x1, Pallas kernels, project_and_reduce(): pl.pallas_call(kernel, out_shape=jax.ShapeDtypeStruct((rows, width), jnp....  58.9 us
    unnamed x12, local copies, waits for them, and re-layouts  8.54 us

profile of v5, /device:TPU:8, one launch (start us, length us, event | category | flops | bytes accessed | tf_op | source)
XLA Modules:
  0.0 153.8 jit_solution(7761692627845233182)
XLA Ops:
  0.0 0.0 copy-start.2
  0.0 0.0 copy-start.1
  0.8 0.1 pad.2.clone
  0.9 0.8 copy.20
  1.6 0.1 iota_compare_fusion
  1.7 0.8 select_reduce_fusion
  2.5 0.1 broadcast_bitcast_fusion
  2.6 0.1 maximum_maximum_fusion
  2.6 0.7 broadcast_in_dim.50.meta_ref
  3.3 1.9 %copy.32 = bf16[256,8,128]{2,0,1:T(8,128)(2,1)} copy(bf16[256,8,128]{2,1,0:T(8,128)(2,1)} %param.18) | data formatting | bytes 1048576 | tf_op args[7]
  5.2 0.0 copy-done.2
  5.2 0.0 copy-start
  5.2 1.1 copy.26
  6.4 0.0 copy-done.1
  6.4 1.3 copy.31
  7.6 0.0 copy-done
  7.6 1.6 %copy.19 = bf16[8,768,128]{1,2,0:T(8,128)(2,1)} copy(bf16[8,768,128]{2,1,0:T(8,128)(2,1)S(1)} %copy-done) | data formatting | bytes 3145728 | tf_op args[2]
  9.2 83.8 %gather_and_attend.1.flat_ref = bf16[256,2048]{1,0:T(8,128)(2,1)} custom-call(s32[8]{0:T(128)} %offsets_ref.1, s32[16]{0:T(128)} %groups_ref.1, bf16[16,256,128]{2,1,0:T(8,128)(2,1)} %bitcast.18, bf16[8,768,128]{2,1,0:T(8,128)(2,1)} %k_ref.1, bf16[8,128,768]{2,1,0:T(8,128)(2,1)} %bitcast.17, f32[24,1,768]{2,1,0:T(1,128)} %broadcast_in_dim.50.meta_ref, ...), custom_call_target="tpu_custom_call" | custom-call | flops 6442450944 | bytes 6291456 | tf_op jit(solution)/shard_map/gather_and_attend/pallas_call | solution.py:501
  93.0 58.9 %project_and_reduce.1 = bf16[256,1024]{1,0:T(8,128)(2,1)} custom-call(bf16[256,2048]{1,0:T(8,128)(2,1)} %gather_and_attend.1.flat_ref, bf16[2048,8192]{1,0:T(8,128)(2,1)} %weight_ref.1), custom_call_target="tpu_custom_call" | custom-call | flops 8589934592 | bytes 33554432 | tf_op jit(solution)/shard_map/project_and_reduce/pallas_call | solution.py:254
  151.9 1.9 %copy.35 = bf16[256,1024]{1,0:T(8,128)(2,1)} copy(bf16[256,1024]{1,0:T(8,128)(2,1)} %project_and_reduce.1) | data formatting | bytes 1048576
  (2 shorter events, 0.0 us)
Async XLA Ops:
  0.0 5.2 %copy-start.2 = (bf16[256,8,128]{2,1,0:T(8,128)(2,1)S(1)}, bf16[256,8,128]{2,1,0:T(8,128)(2,1)}, u32[]{:S(2)}) copy-start(bf16[256,8,128]{2,1,0:T(8,128)(2,1)} %param.19) | copy-start | bytes 1572868
  0.0 6.4 %copy-start.1 = (bf16[256,16,128]{2,1,0:T(8,128)(2,1)S(1)}, bf16[256,16,128]{2,1,0:T(8,128)(2,1)}, u32[]{:S(2)}) copy-start(bf16[256,16,128]{2,1,0:T(8,128)(2,1)} %param.11) | copy-start | bytes 3145732
  5.2 2.4 %copy-start = (bf16[8,768,128]{2,1,0:T(8,128)(2,1)S(1)}, bf16[8,768,128]{2,1,0:T(8,128)(2,1)}, u32[]{:S(2)}) copy-start(bf16[8,768,128]{2,1,0:T(8,128)(2,1)} %param.13) | copy-start | bytes 4718596

commit v6 on v4

--- a/solution.py
+++ b/solution.py
@@ -278,6 +278,7 @@
     near = group_count // 2
     spans_here = row_count // SPAN
     factor = LOG2E / math.sqrt(head_width)
+    together = math.gcd(heads_here, 4)
 
     def kernel(
         offsets_ref, groups_ref, q_ref, k_ref, v_ref, meta_ref, fk_ref, fv_ref, out_ref,
@@ -383,7 +384,7 @@
                 part = meta_of[row, :, pl.ds(offset + j * SPAN, SPAN)]
                 return jnp.concatenate([part] * spans_here, axis=1)
 
-            def one(h, carry):
+            def one(h):
                 g = groups_ref[h]
                 raw = lax.dot_general(
                     keys_of(g), q_ref[h], (((1,), (1,)), ((), ())),
@@ -405,20 +406,30 @@
                     expo = jnp.exp2(score - largest)
                     added = added + jnp.sum(expo, axis=0, keepdims=True)
                     weights.append((expo * scales(g + group_count, j)).astype(jnp.bfloat16))
-                top[h] = largest
-                total[h] = added
-                mixed[h] = mixed[h] * keep + jnp.dot(
+                summed = mixed[h] * keep + jnp.dot(
                     values_of(g), jnp.concatenate(weights, axis=0),
                     preferred_element_type=jnp.float32,
                 )
+                return h, largest, added, summed
+
+            def several(i, carry):
+                done = [one(i * together + j) for j in range(together)]
+                for h, largest, added, summed in done:
+                    top[h] = largest
+                    total[h] = added
+                    mixed[h] = summed
                 return carry
 
-            lax.fori_loop(0, heads_here, one, 0, unroll=2)
+            lax.fori_loop(0, heads_here // together, several, 0)
 
         def attend_ref(b, offset, k, v):
             attend(b, offset, half, lambda g: k[g], lambda g: v[g])
 
-        attend(0, 0, slot_count, lambda g: k_ref[g], lambda g: v_ref[g])
+        def attend_own(offset):
+            slots = pl.ds(offset, half)
+            attend(0, offset, half, lambda g: k_ref[g, slots], lambda g: v_ref[g, :, slots])
+
+        attend_own(0)
 
         def share(pairs):
             return [copy(ref.at[part], ref.at[part], sibling) for ref, part in pairs]
@@ -435,8 +446,8 @@
                 (xf_v, dn_v, low, to_y), (yf_v, dn_v, high, to_x),
             )
         ]
-        arrived(share([(xf_k, mine), (xf_v, mine), (yf_k, mine), (yf_v, mine)]))
-        attend_ref(1, first, xf_k, xf_v)
+        first_shared = share([(xf_k, mine), (xf_v, mine), (yf_k, mine), (yf_v, mine)])
+        attend_own(half)
         seconds = [
             copy(own(ref, second), target.at[mine], device)
             for ref, tx, ty in ((k_ref, xs_k, ys_k), (v_ref, xs_v, ys_v))
@@ -449,15 +460,17 @@
             for part in (low, high)
         ]
         near_shared = share([(dn_k, mine), (dn_v, mine)])
+        arrived(first_shared)
+        attend_ref(1, first, xf_k, xf_v)
         attend_ref(2, first, yf_k, yf_v)
+        arrived(seconds)
+        second_shared = share([(xs_k, mine), (xs_v, mine), (ys_k, mine), (ys_v, mine)])
         arrived(near_shared)
         attend_ref(3, first, dn_k, dn_v)
-        arrived(seconds)
-        second_shared = share([(xs_k, mine), (xs_v, mine), (ys_k, mine), (ys_v, mine)])
+        arrived(across)
+        far_shared = share([(df_k, mine), (df_v, mine)])
         arrived(second_shared)
         attend_ref(1, second, xs_k, xs_v)
-        arrived(across)
-        far_shared = share([(df_k, mine), (df_v, mine)])
         attend_ref(2, second, ys_k, ys_v)
         arrived(far_shared)
         attend_ref(3, second, df_k, df_v)

time: 145 us -> 144 us (level)
  no operation moved by 1% of the time
where the time goes in v6:
time: 144 us
  Pallas kernels  133 us (92%)
  local copies, waits for them, and re-layouts  9.36 us (6%)
    pallas_call x1, Pallas kernels, gather_and_attend(): pl.pallas_call(kernel, out_shape=jax.ShapeDtypeStruct((row_count, heads_h...  81.4 us
    pallas_call x1, Pallas kernels, project_and_reduce(): pl.pallas_call(kernel, out_shape=jax.ShapeDtypeStruct((rows, width), jnp....  51.6 us
    unnamed x12, local copies, waits for them, and re-layouts  8.54 us

profile of v6, /device:TPU:8, one launch (start us, length us, event | category | flops | bytes accessed | tf_op | source)
XLA Modules:
  0.0 144.1 jit_solution(2957952288588744570)
XLA Ops:
  0.0 0.0 copy-start.2
  0.0 0.0 copy-start.1
  0.8 0.1 pad.2.clone
  0.9 0.8 copy.20
  1.6 0.1 iota_compare_fusion
  1.7 0.8 select_reduce_fusion
  2.5 0.1 broadcast_bitcast_fusion
  2.6 0.1 maximum_maximum_fusion
  2.6 0.7 broadcast_in_dim.50.meta_ref
  3.3 1.9 %copy.32 = bf16[256,8,128]{2,0,1:T(8,128)(2,1)} copy(bf16[256,8,128]{2,1,0:T(8,128)(2,1)} %param.18) | data formatting | bytes 1048576 | tf_op args[7]
  5.2 0.0 copy-done.2
  5.2 0.0 copy-start
  5.2 1.1 copy.26
  6.4 0.0 copy-done.1
  6.4 1.3 copy.31
  7.6 0.0 copy-done
  7.6 1.6 %copy.19 = bf16[8,768,128]{1,2,0:T(8,128)(2,1)} copy(bf16[8,768,128]{2,1,0:T(8,128)(2,1)S(1)} %copy-done) | data formatting | bytes 3145728 | tf_op args[2]
  9.2 81.4 %gather_and_attend.1.flat_ref = bf16[256,2048]{1,0:T(8,128)(2,1)} custom-call(s32[8]{0:T(128)} %offsets_ref.1, s32[16]{0:T(128)} %groups_ref.1, bf16[16,256,128]{2,1,0:T(8,128)(2,1)} %bitcast.18, bf16[8,768,128]{2,1,0:T(8,128)(2,1)} %k_ref.1, bf16[8,128,768]{2,1,0:T(8,128)(2,1)} %bitcast.17, f32[24,1,768]{2,1,0:T(1,128)} %broadcast_in_dim.50.meta_ref, ...), custom_call_target="tpu_custom_call" | custom-call | flops 6442450944 | bytes 6291456 | tf_op jit(solution)/shard_map/gather_and_attend/pallas_call | solution.py:494
  90.6 51.6 %project_and_reduce.1 = bf16[256,1024]{1,0:T(8,128)(2,1)} custom-call(bf16[256,2048]{1,0:T(8,128)(2,1)} %gather_and_attend.1.flat_ref, bf16[2048,8192]{1,0:T(8,128)(2,1)} %weight_ref.1), custom_call_target="tpu_custom_call" | custom-call | flops 8589934592 | bytes 33554432 | tf_op jit(solution)/shard_map/project_and_reduce/pallas_call | solution.py:240
  142.2 1.9 %copy.35 = bf16[256,1024]{1,0:T(8,128)(2,1)} copy(bf16[256,1024]{1,0:T(8,128)(2,1)} %project_and_reduce.1) | data formatting | bytes 1048576
  (2 shorter events, 0.0 us)
Async XLA Ops:
  0.0 5.2 %copy-start.2 = (bf16[256,8,128]{2,1,0:T(8,128)(2,1)S(1)}, bf16[256,8,128]{2,1,0:T(8,128)(2,1)}, u32[]{:S(2)}) copy-start(bf16[256,8,128]{2,1,0:T(8,128)(2,1)} %param.19) | copy-start | bytes 1572868
  0.0 6.4 %copy-start.1 = (bf16[256,16,128]{2,1,0:T(8,128)(2,1)S(1)}, bf16[256,16,128]{2,1,0:T(8,128)(2,1)}, u32[]{:S(2)}) copy-start(bf16[256,16,128]{2,1,0:T(8,128)(2,1)} %param.11) | copy-start | bytes 3145732
  5.2 2.4 %copy-start = (bf16[8,768,128]{2,1,0:T(8,128)(2,1)S(1)}, bf16[8,768,128]{2,1,0:T(8,128)(2,1)}, u32[]{:S(2)}) copy-start(bf16[8,768,128]{2,1,0:T(8,128)(2,1)} %param.13) | copy-start | bytes 4718596
